TPU v7x, 32 devices: a whole 2x2x4 slice. The times are simulated.
32 devices in a mesh: rep: 4 (over y, core), shard: 8 (over z, x).
Axes of the slice: x: 2, y: 2, z: 4, core: 2. Of those that a mesh axis runs over, the one named last changes fastest.
Arguments:
- hidden_in: bfloat16 [8192, 1536], P(('rep', 'shard')), may hold values from -6 to 6
- segments: int32 [32, 256], P(('rep', 'shard')), may hold values from 0 to 63, never falling along the last dimension, each value on 1 to 128 neighbouring positions
- routes: int32 [8192, 4], P(('rep', 'shard')), may hold values from 0 to 7, all different within a row; in each aligned block of 256 rows (0 to 255, 256 to 511, ...) at most 192 rows name the same one
- gate_weights: float32 [8192, 4], P(('rep', 'shard')), may hold values from 0.2 to 0.6
- grad_out: bfloat16 [8192, 1536], P(('rep', 'shard')), may hold values from -6 to 6
- attn_gain: bfloat16 [1536], P('shard'), may hold values from 0.5 to 1.5
- query_weight: bfloat16 [1536, 1536], P('shard'), may hold values from -0.3125 to 0.3125
- key_weight: bfloat16 [1536, 256], P('shard'), may hold values from -0.15625 to 0.15625
- value_weight: bfloat16 [1536, 256], P('shard'), may hold values from -0.15625 to 0.15625
- output_weight: bfloat16 [1536, 1536], P('shard'), may hold values from -0.875 to 0.875
- ffn_gain: bfloat16 [1536], P('shard'), may hold values from 0.5 to 1.5
- gate_weight: bfloat16 [8, 1536, 768], P(None, 'shard'), may hold values from -0.15625 to 0.15625
- up_weight: bfloat16 [8, 1536, 768], P(None, 'shard'), may hold values from -0.15625 to 0.15625
- down_weight: bfloat16 [8, 768, 1536], P(None, 'shard'), may hold values from -0.4375 to 0.4375
Outputs:
- layer_out: bfloat16 [8192, 1536], P(('rep', 'shard'))
- grad_in: bfloat16 [8192, 1536], P(('rep', 'shard'))
- grad_attn_gain: float32 [1536], P('shard')
- grad_query_weight: float32 [1536, 1536], P('shard')
- grad_key_weight: float32 [1536, 256], P('shard')
- grad_value_weight: float32 [1536, 256], P('shard')
- grad_output_weight: float32 [1536, 1536], P('shard')
- grad_ffn_gain: float32 [1536], P('shard')
- grad_gate_weight: float32 [8, 1536, 768], P(None, 'shard')
- grad_up_weight: float32 [8, 1536, 768], P(None, 'shard')
- grad_down_weight: float32 [8, 768, 1536], P(None, 'shard')
Inputs may be any that keep to these rules, and one draw needn't show every extreme that they name: `routes`: in the 256 rows of one sequence no expert is named by more than 192 rows; a row's experts differ. `segments`: document numbers never fall along a sequence; a document holds 1 to 128 tokens.
All inputs are finite; a program needn't handle non-finite values.
Results may differ from a plain program's by a relative error of at most 0.014.
Values may be sent and summed in bfloat16 or wider, within the bound.
A program may use at most 320 MiB of HBM per device.

v0:
```python
import jax
import jax.numpy as jnp
from jax import lax
from jax.sharding import PartitionSpec as P

HEADS = 12
KV_HEADS = 2
HEAD_DIM = 128
EXPERTS = 8
CAP = 192


epsilon = 1e-06
rotary_base = 1000000.0
masked_score = -1e30


def rms_norm(values, scale_gain):
    return (
        values * lax.rsqrt(jnp.mean(values * values, axis=-1, keepdims=True) + epsilon) * scale_gain
    )


def norm_back(values, scale_gain, upstream):
    inverse = lax.rsqrt(jnp.mean(values * values, axis=-1, keepdims=True) + epsilon)
    normal = values * inverse
    gain_grad = jnp.sum(upstream * normal, axis=0)
    scaled = upstream * scale_gain
    value_grad = inverse * (scaled - normal * jnp.mean(scaled * normal, axis=-1, keepdims=True))
    return (value_grad, gain_grad)


def rotary_tables(length, head_width):
    half_width = head_width // 2
    frequency = rotary_base ** (-2.0 * jnp.arange(half_width, dtype=jnp.float32) / head_width)
    angles = jnp.arange(length, dtype=jnp.float32)[:, None] * frequency[None, :]
    return (jnp.cos(angles)[:, None, :], jnp.sin(angles)[:, None, :])


def rotate(values, cosine, sine_table):
    half_width = values.shape[-1] // 2
    first_half = values[..., :half_width]
    second_half = values[..., half_width:]
    return jnp.concatenate(
        [
            first_half * cosine - second_half * sine_table,
            second_half * cosine + first_half * sine_table,
        ],
        axis=-1,
    )


def unrotate(values, cosine, sine_table):
    half_width = values.shape[-1] // 2
    first_half = values[..., :half_width]
    second_half = values[..., half_width:]
    return jnp.concatenate(
        [
            first_half * cosine + second_half * sine_table,
            second_half * cosine - first_half * sine_table,
        ],
        axis=-1,
    )


def dispatch(routes, experts, capacity):
    flat_routes = routes.reshape(-1)
    onehot = (flat_routes[:, None] == jnp.arange(experts, dtype=jnp.int32)[None, :]).astype(
        jnp.int32
    )
    slot_rank = jnp.sum((jnp.cumsum(onehot, axis=0) - 1) * onehot, axis=1)
    owners = jnp.arange(flat_routes.shape[0], dtype=jnp.int32) // routes.shape[1]
    slot_table = jnp.zeros((experts, capacity), jnp.int32).at[flat_routes, slot_rank].set(owners)
    slot_index = (flat_routes * capacity + slot_rank).reshape(routes.shape)
    return (slot_table, slot_index)


def unpack_attention(gathered):
    gain_first, query_full, key_full, value_full, output_full, gain_second = gathered
    return (
        gain_first.astype(jnp.float32),
        query_full,
        key_full,
        value_full,
        output_full,
        gain_second.astype(jnp.float32),
    )


def shards(
    hidden_in,
    segments,
    routes,
    gate_weights,
    grad_out,
    attn_gain,
    query_weight,
    key_weight,
    value_weight,
    output_weight,
    ffn_gain,
    gate_weight,
    up_weight,
    down_weight,
):
    length, model_width = hidden_in.shape
    groups = HEADS // KV_HEADS
    factor = HEAD_DIM ** (-0.5)
    attn_full = (
        lax.all_gather(attn_gain, "shard", axis=0, tiled=True),
        lax.all_gather(query_weight, "shard", axis=0, tiled=True),
        lax.all_gather(key_weight, "shard", axis=0, tiled=True),
        lax.all_gather(value_weight, "shard", axis=0, tiled=True),
        lax.all_gather(output_weight, "shard", axis=0, tiled=True),
        lax.all_gather(ffn_gain, "shard", axis=0, tiled=True),
    )
    gate_full, up_full, down_full = (
        lax.all_gather(gate_weight, "shard", axis=1, tiled=True),
        lax.all_gather(up_weight, "shard", axis=1, tiled=True),
        lax.all_gather(down_weight, "shard", axis=1, tiled=True),
    )
    gain_first, query_full, key_full, value_full, output_full, gain_second = unpack_attention(
        attn_full
    )
    inputs = hidden_in.astype(jnp.float32)
    normed = rms_norm(inputs, gain_first).astype(jnp.bfloat16)
    query_raw = jnp.dot(normed, query_full, preferred_element_type=jnp.float32)
    key_raw = jnp.dot(normed, key_full, preferred_element_type=jnp.float32)
    value_heads = (
        jnp.dot(normed, value_full, preferred_element_type=jnp.float32)
        .astype(jnp.bfloat16)
        .reshape(length, KV_HEADS, HEAD_DIM)
    )
    cosine, sine_table = rotary_tables(length, HEAD_DIM)
    rotated_queries = rotate(query_raw.reshape(length, HEADS, HEAD_DIM), cosine, sine_table).astype(
        jnp.bfloat16
    )
    rotated_keys = rotate(key_raw.reshape(length, KV_HEADS, HEAD_DIM), cosine, sine_table).astype(
        jnp.bfloat16
    )
    grouped = rotated_queries.reshape(length, KV_HEADS, groups, HEAD_DIM)
    segment = segments[0]
    position = jnp.arange(length, dtype=jnp.int32)
    allowed = (position[:, None] >= position[None, :]) & (segment[:, None] == segment[None, :])
    scores = (
        jnp.einsum("ikgd,jkd->kgij", grouped, rotated_keys, preferred_element_type=jnp.float32)
        * factor
    )
    scores = jnp.where(allowed, scores, masked_score)
    top_score = jnp.max(scores, axis=-1, keepdims=True)
    exponent_terms = jnp.exp(scores - top_score)
    probability = exponent_terms / jnp.sum(exponent_terms, axis=-1, keepdims=True)
    probability_low = probability.astype(jnp.bfloat16)
    attended = jnp.einsum(
        "kgij,jkd->ikgd", probability_low, value_heads, preferred_element_type=jnp.float32
    )
    attended = attended.reshape(length, HEADS * HEAD_DIM).astype(jnp.bfloat16)
    mixed = inputs + jnp.dot(attended, output_full, preferred_element_type=jnp.float32)
    normed_two = rms_norm(mixed, gain_second).astype(jnp.bfloat16)
    slot_table, slot_index = dispatch(routes, EXPERTS, CAP)
    gathered_rows = normed_two[slot_table]
    gate_proj = jnp.einsum(
        "ecd,edf->ecf", gathered_rows, gate_full, preferred_element_type=jnp.float32
    )
    up_proj = jnp.einsum("ecd,edf->ecf", gathered_rows, up_full, preferred_element_type=jnp.float32)
    hidden_act = (jax.nn.silu(gate_proj) * up_proj).astype(jnp.bfloat16)
    expert_out = jnp.einsum(
        "ecf,efd->ecd", hidden_act, down_full, preferred_element_type=jnp.float32
    ).reshape(EXPERTS * CAP, model_width)
    picked = expert_out[slot_index]
    layer_out = (mixed + jnp.sum(gate_weights[:, :, None] * picked, axis=1)).astype(jnp.bfloat16)
    tied = lax.optimization_barrier(
        (layer_out, attn_gain, query_weight, key_weight, value_weight, output_weight, ffn_gain)
    )
    attn_again = (
        lax.all_gather(tied[1], "shard", axis=0, tiled=True),
        lax.all_gather(tied[2], "shard", axis=0, tiled=True),
        lax.all_gather(tied[3], "shard", axis=0, tiled=True),
        lax.all_gather(tied[4], "shard", axis=0, tiled=True),
        lax.all_gather(tied[5], "shard", axis=0, tiled=True),
        lax.all_gather(tied[6], "shard", axis=0, tiled=True),
    )
    gain_first, query_full, key_full, value_full, output_full, gain_second = unpack_attention(
        attn_again
    )
    upstream = grad_out.astype(jnp.float32)
    spread = (gate_weights[:, :, None] * upstream[:, None, :]).reshape(-1, model_width)
    expert_grad = (
        jnp.zeros((EXPERTS * CAP, model_width), jnp.float32).at[slot_index.reshape(-1)].set(spread)
    )
    expert_grad = expert_grad.astype(jnp.bfloat16)
    bound = lax.optimization_barrier((layer_out, gate_weight, up_weight, down_weight))
    gate_full, up_full, down_full = (
        lax.all_gather(bound[1], "shard", axis=1, tiled=True),
        lax.all_gather(bound[2], "shard", axis=1, tiled=True),
        lax.all_gather(bound[3], "shard", axis=1, tiled=True),
    )
    block_grad = expert_grad.reshape(EXPERTS, CAP, model_width)
    hidden_grad = jnp.einsum(
        "ecd,efd->ecf", block_grad, down_full, preferred_element_type=jnp.float32
    )
    down_weight_grad = jnp.einsum(
        "ecf,ecd->efd", hidden_act, block_grad, preferred_element_type=jnp.float32
    )
    sigmoid_gate = jax.nn.sigmoid(gate_proj)
    gate_grad = (
        hidden_grad * up_proj * sigmoid_gate * (1.0 + gate_proj * (1.0 - sigmoid_gate))
    ).astype(jnp.bfloat16)
    up_grad = (hidden_grad * jax.nn.silu(gate_proj)).astype(jnp.bfloat16)
    rows_grad = jnp.einsum("ecf,edf->ecd", gate_grad, gate_full, preferred_element_type=jnp.float32)
    rows_grad = rows_grad + jnp.einsum(
        "ecf,edf->ecd", up_grad, up_full, preferred_element_type=jnp.float32
    )
    gate_weight_grad = jnp.einsum(
        "ecd,ecf->edf", gathered_rows, gate_grad, preferred_element_type=jnp.float32
    )
    up_weight_grad = jnp.einsum(
        "ecd,ecf->edf", gathered_rows, up_grad, preferred_element_type=jnp.float32
    )
    share_gate, share_up, share_down = (
        lax.psum_scatter(gate_weight_grad, "shard", scatter_dimension=1, tiled=True),
        lax.psum_scatter(up_weight_grad, "shard", scatter_dimension=1, tiled=True),
        lax.psum_scatter(down_weight_grad, "shard", scatter_dimension=1, tiled=True),
    )
    normed_two_grad = (
        jnp.zeros((length, model_width), jnp.float32)
        .at[slot_table.reshape(-1)]
        .add(rows_grad.reshape(-1, model_width))
    )
    mixed_part, ffn_gain_grad = norm_back(mixed, gain_second, normed_two_grad)
    mixed_grad = upstream + mixed_part
    mixed_low = mixed_grad.astype(jnp.bfloat16)
    output_weight_grad = jnp.einsum(
        "lq,ld->qd", attended, mixed_low, preferred_element_type=jnp.float32
    )
    attended_grad = jnp.einsum(
        "ld,qd->lq", mixed_low, output_full, preferred_element_type=jnp.float32
    )
    attended_grad = attended_grad.astype(jnp.bfloat16).reshape(length, KV_HEADS, groups, HEAD_DIM)
    prob_grad = jnp.einsum(
        "ikgd,jkd->kgij", attended_grad, value_heads, preferred_element_type=jnp.float32
    )
    value_grad = jnp.einsum(
        "kgij,ikgd->jkd", probability_low, attended_grad, preferred_element_type=jnp.float32
    )
    value_grad = value_grad.astype(jnp.bfloat16).reshape(length, KV_HEADS * HEAD_DIM)
    score_grad = (
        probability * (prob_grad - jnp.sum(probability * prob_grad, axis=-1, keepdims=True))
    ).astype(jnp.bfloat16)
    query_rot_grad = (
        jnp.einsum("kgij,jkd->ikgd", score_grad, rotated_keys, preferred_element_type=jnp.float32)
        * factor
    )
    key_rot_grad = (
        jnp.einsum("kgij,ikgd->jkd", score_grad, grouped, preferred_element_type=jnp.float32)
        * factor
    )
    query_raw_grad = unrotate(query_rot_grad.reshape(length, HEADS, HEAD_DIM), cosine, sine_table)
    query_raw_grad = query_raw_grad.astype(jnp.bfloat16).reshape(length, HEADS * HEAD_DIM)
    key_raw_grad = (
        unrotate(key_rot_grad, cosine, sine_table)
        .astype(jnp.bfloat16)
        .reshape(length, KV_HEADS * HEAD_DIM)
    )
    normed_grad = jnp.einsum(
        "lq,dq->ld", query_raw_grad, query_full, preferred_element_type=jnp.float32
    )
    normed_grad = normed_grad + jnp.einsum(
        "lq,dq->ld", key_raw_grad, key_full, preferred_element_type=jnp.float32
    )
    normed_grad = normed_grad + jnp.einsum(
        "lq,dq->ld", value_grad, value_full, preferred_element_type=jnp.float32
    )
    query_weight_grad = jnp.einsum(
        "ld,lq->dq", normed, query_raw_grad, preferred_element_type=jnp.float32
    )
    key_weight_grad = jnp.einsum(
        "ld,lq->dq", normed, key_raw_grad, preferred_element_type=jnp.float32
    )
    value_weight_grad = jnp.einsum(
        "ld,lq->dq", normed, value_grad, preferred_element_type=jnp.float32
    )
    input_part, attn_gain_grad = norm_back(inputs, gain_first, normed_grad)
    grad_in = (mixed_grad + input_part).astype(jnp.bfloat16)
    share_gain_one, share_query, share_key, share_value, share_output, share_gain_two = (
        lax.psum_scatter(attn_gain_grad, "shard", scatter_dimension=0, tiled=True),
        lax.psum_scatter(query_weight_grad, "shard", scatter_dimension=0, tiled=True),
        lax.psum_scatter(key_weight_grad, "shard", scatter_dimension=0, tiled=True),
        lax.psum_scatter(value_weight_grad, "shard", scatter_dimension=0, tiled=True),
        lax.psum_scatter(output_weight_grad, "shard", scatter_dimension=0, tiled=True),
        lax.psum_scatter(ffn_gain_grad, "shard", scatter_dimension=0, tiled=True),
    )
    total_gain_one, total_query, total_key, total_value, total_output, total_gain_two = lax.psum(
        (share_gain_one, share_query, share_key, share_value, share_output, share_gain_two), "rep"
    )
    total_gate, total_up, total_down = lax.psum((share_gate, share_up, share_down), "rep")
    return (
        layer_out,
        grad_in,
        total_gain_one,
        total_query,
        total_key,
        total_value,
        total_output,
        total_gain_two,
        total_gate,
        total_up,
        total_down,
    )


def solution(mesh):
    return jax.shard_map(
        shards,
        mesh=mesh,
        in_specs=(
            P(("rep", "shard"), None),
            P(("rep", "shard"), None),
            P(("rep", "shard"), None),
            P(("rep", "shard"), None),
            P(("rep", "shard"), None),
            P("shard"),
            P("shard", None),
            P("shard", None),
            P("shard", None),
            P("shard", None),
            P("shard"),
            P(None, "shard", None),
            P(None, "shard", None),
            P(None, "shard", None),
        ),
        out_specs=(
            P(("rep", "shard"), None),
            P(("rep", "shard"), None),
            P("shard"),
            P("shard", None),
            P("shard", None),
            P("shard", None),
            P("shard", None),
            P("shard"),
            P(None, "shard", None),
            P(None, "shard", None),
            P(None, "shard", None),
        ),
        check_vma=False,
    )
```

profile of v0, /device:TPU:13, one launch (start us, length us, event | category | flops | bytes accessed | tf_op | source)
XLA Modules:
  0.0 5208.5 jit_solution(2923870295415149534)
XLA Ops:
  29.9 29.7 all_gather.56
  73.4 27.7 all_gather.55
  116.2 70.2 %all-gather.13.cloned.1.call-done = bf16[1536,1536]{1,0:T(8,128)(2,1)} async-done(((bf16[192,1536]{1,0:T(8,128)(2,1)}), bf16[1536,1536]{1,0:T(8,128)(2,1)}) %all-gather.13.cloned.1.call-update) | async-done | bytes 4718608 | tf_op jit(solution)/shard_map/all_gather | solution.py:114
  196.9 353.9 %all-gather.15.cloned.1.call-done = bf16[8,1536,768]{2,1,0:T(8,128)(2,1)} async-done(((bf16[8,192,768]{2,1,0:T(8,128)(2,1)}), bf16[8,1536,768]{2,1,0:T(8,128)(2,1)}) %all-gather.15.cloned.1.call-update) | async-done | bytes 18874384 | tf_op jit(solution)/shard_map/all_gather | solution.py:118
  564.6 350.0 %all-gather.17.cloned.1.call-done = bf16[8,1536,768]{2,1,0:T(8,128)(2,1)} async-done(((bf16[8,192,768]{2,1,0:T(8,128)(2,1)}), bf16[8,1536,768]{2,1,0:T(8,128)(2,1)}) %all-gather.17.cloned.1.call-update) | async-done | bytes 18874384 | tf_op jit(solution)/shard_map/all_gather | solution.py:119
  930.9 347.6 %all-gather.19.cloned.1.call-done = bf16[8,768,1536]{2,1,0:T(8,128)(2,1)} async-done(((bf16[8,96,1536]{2,1,0:T(8,128)(2,1)}), bf16[8,768,1536]{2,1,0:T(8,128)(2,1)}) %all-gather.19.cloned.1.call-update) | async-done | bytes 18874384 | tf_op jit(solution)/shard_map/all_gather | solution.py:120
  1352.7 21.5 all-reduce.9
  1374.2 310.7 %all-gather.21.cloned.1.call-done = bf16[8,768,1536]{2,1,0:T(8,128)(2,1)} async-done(((bf16[8,96,1536]{2,1,0:T(8,128)(2,1)}), bf16[8,768,1536]{2,1,0:T(8,128)(2,1)}) %all-gather.21.cloned.1.call-update) | async-done | bytes 18874384 | tf_op jit(solution)/shard_map/all_gather | solution.py:196
  1701.6 347.4 %all-gather.23.cloned.1.call-done = bf16[8,1536,768]{2,1,0:T(8,128)(2,1)} async-done(((bf16[8,192,768]{2,1,0:T(8,128)(2,1)}), bf16[8,1536,768]{2,1,0:T(8,128)(2,1)}) %all-gather.23.cloned.1.call-update) | async-done | bytes 18874384 | tf_op jit(solution)/shard_map/all_gather | solution.py:194
  2061.9 351.0 %all-gather.25.cloned.1.call-done = bf16[8,1536,768]{2,1,0:T(8,128)(2,1)} async-done(((bf16[8,192,768]{2,1,0:T(8,128)(2,1)}), bf16[8,1536,768]{2,1,0:T(8,128)(2,1)}) %all-gather.25.cloned.1.call-update) | async-done | bytes 18874384 | tf_op jit(solution)/shard_map/all_gather | solution.py:195
  2428.1 17.9 scatter_custom_fusion.1
  2449.7 43.2 all-gather.27.cloned.1.call-done
  2524.1 17.3 fusion.71
  2578.9 56.7 %reduce-scatter.12.cloned.1.call-done = f32[192,256]{1,0:T(8,128)} async-done(((f32[1536,256]{1,0:T(8,128)}), f32[192,256]{1,0:T(8,128)}) %reduce-scatter.12.cloned.1.call-update) | async-done | bytes 196624 | tf_op jit(solution)/shard_map/reduce_scatter | solution.py:289
  2635.7 166.0 %reduce-scatter.8.cloned.1.call-done = f32[192,1536]{1,0:T(8,128)} async-done(((f32[1536,1536]{1,0:T(8,128)}), f32[192,1536]{1,0:T(8,128)}) %reduce-scatter.8.cloned.1.call-update) | async-done | bytes 1179664 | tf_op jit(solution)/shard_map/reduce_scatter | solution.py:287
  2801.7 166.0 %reduce-scatter.14.cloned.1.call-done = f32[192,1536]{1,0:T(8,128)} async-done(((f32[1536,1536]{1,0:T(8,128)}), f32[192,1536]{1,0:T(8,128)}) %reduce-scatter.14.cloned.1.call-update) | async-done | bytes 1179664 | tf_op jit(solution)/shard_map/reduce_scatter | solution.py:290
  2967.7 608.0 %reduce-scatter.20.cloned.1.call-done = f32[8,96,1536]{2,1,0:T(8,128)} async-done(((f32[8,768,1536]{2,1,0:T(8,128)}), f32[8,96,1536]{2,1,0:T(8,128)}) %reduce-scatter.20.cloned.1.call-update) | async-done | bytes 4718608 | tf_op jit(solution)/shard_map/reduce_scatter | solution.py:223
  3575.7 608.4 %reduce-scatter.16.cloned.1.call-done = f32[8,192,768]{2,1,0:T(8,128)} async-done(((f32[8,1536,768]{2,1,0:T(8,128)}), f32[8,192,768]{2,1,0:T(8,128)}) %reduce-scatter.16.cloned.1.call-update) | async-done | bytes 4718608 | tf_op jit(solution)/shard_map/reduce_scatter | solution.py:221
  4184.1 607.7 %reduce-scatter.18.cloned.1.call-done = f32[8,192,768]{2,1,0:T(8,128)} async-done(((f32[8,1536,768]{2,1,0:T(8,128)}), f32[8,192,768]{2,1,0:T(8,128)}) %reduce-scatter.18.cloned.1.call-update) | async-done | bytes 4718608 | tf_op jit(solution)/shard_map/reduce_scatter | solution.py:222
  4792.7 28.4 all_gather.69
  4821.1 29.3 all_gather.70
  4850.4 37.0 all-gather.29.cloned.1.call-done
  4893.5 25.9 all-reduce.6
  4936.1 248.2 %all-reduce.13.cloned.1.call-done = (f32[192,1536]{1,0:T(8,128)}, f32[192,256]{1,0:T(8,128)}, f32[192,256]{1,0:T(8,128)}, f32[192,1536]{1,0:T(8,128)}, f32[8,192...) async-done(((f32[192,1536]{1,0:T(8,128)}, f32[192,256]{1,0:T(8,128)}, f32[192,256]{1,0:T(8,128)}, f32[192,1536]{1,0:T(8,128)}, ...) | async-done | bytes 16908304 | tf_op jit(solution)/shard_map/psum | solution.py:293
  (258 shorter events, 321.7 us)
Async XLA Ops:
  7.2 96.7 %all-gather.11.cloned.1.call-start = ((), (), s32[]{:S(2)}) async-start(), calls=%async_computation.7 | async-start | bytes 5308416 | tf_op jit(solution)/shard_map/all_gather | solution.py:111
  7.9 178.5 %all-gather.13.cloned.1.call-start = ((), (), s32[]{:S(2)}) async-start(), calls=%async_computation.8 | async-start | bytes 5308416 | tf_op jit(solution)/shard_map/all_gather | solution.py:114
  8.7 542.1 %all-gather.15.cloned.1.call-start = ((), (), s32[]{:S(2)}) async-start(), calls=%async_computation.9 | async-start | bytes 21233664 | tf_op jit(solution)/shard_map/all_gather | solution.py:118
  9.5 905.2 %all-gather.17.cloned.1.call-start = ((), (), s32[]{:S(2)}) async-start(), calls=%async_computation.10 | async-start | bytes 21233664 | tf_op jit(solution)/shard_map/all_gather | solution.py:119
  10.0 1268.4 %all-gather.19.cloned.1.call-start = ((), (), s32[]{:S(2)}) async-start(), calls=%async_computation.11 | async-start | bytes 21233664 | tf_op jit(solution)/shard_map/all_gather | solution.py:120
  10.6 1674.3 %all-gather.21.cloned.1.call-start = ((), (), s32[]{:S(2)}) async-start(), calls=%async_computation.12 | async-start | bytes 21233664 | tf_op jit(solution)/shard_map/all_gather | solution.py:196
  61.1 47.2 copy-start.19
  61.1 47.2 copy-start.21
  61.2 47.1 copy-start.24
  61.3 47.0 copy-start.26
  116.2 74.1 %copy-start.7 = (bf16[2,128,6,256]{3,1,2,0:T(8,128)(2,1)}, bf16[2,128,6,256]{3,1,2,0:T(8,128)(2,1)S(1)}, u32[]{:S(2)}) copy-start(bf16[2,128,6,256]{3,1,2,0:T(8,128)(2,1)S(1)} %convolution_convert_fusion.1) | copy-start | bytes 2359300
  1321.1 727.8 %all-gather.23.cloned.1.call-start = ((), (), s32[]{:S(2)}) async-start(), calls=%async_computation.13 | async-start | bytes 21233664 | tf_op jit(solution)/shard_map/all_gather | solution.py:194
  1321.9 1091.1 %all-gather.25.cloned.1.call-start = ((), (), s32[]{:S(2)}) async-start(), calls=%async_computation.14 | async-start | bytes 21233664 | tf_op jit(solution)/shard_map/all_gather | solution.py:195
  1322.6 1170.2 %all-gather.27.cloned.1.call-start = ((), (), s32[]{:S(2)}) async-start(), calls=%async_computation.15 | async-start | bytes 5308416 | tf_op jit(solution)/shard_map/all_gather | solution.py:180
  1323.3 1255.6 %reduce-scatter.10.cloned.1.call-start = ((), (), s32[]{:S(2)}) async-start(), calls=%async_computation.18 | async-start | bytes 1769472 | tf_op jit(solution)/shard_map/reduce_scatter | solution.py:288
  2504.6 131.1 %reduce-scatter.12.cloned.1.call-start = ((), (), s32[]{:S(2)}) async-start(), calls=%async_computation.19 | async-start | bytes 1769472 | tf_op jit(solution)/shard_map/reduce_scatter | solution.py:289
  2509.0 292.7 %reduce-scatter.8.cloned.1.call-start = ((), (), s32[]{:S(2)}) async-start(), calls=%async_computation.17 | async-start | bytes 10616832 | tf_op jit(solution)/shard_map/reduce_scatter | solution.py:287
  2515.8 451.9 %reduce-scatter.14.cloned.1.call-start = ((), (), s32[]{:S(2)}) async-start(), calls=%async_computation.20 | async-start | bytes 10616832 | tf_op jit(solution)/shard_map/reduce_scatter | solution.py:290
  2522.4 1053.2 %reduce-scatter.20.cloned.1.call-start = ((), (), s32[]{:S(2)}) async-start(), calls=%async_computation.23 | async-start | bytes 42467328 | tf_op jit(solution)/shard_map/reduce_scatter | solution.py:223
  2541.5 1642.6 %reduce-scatter.16.cloned.1.call-start = ((), (), s32[]{:S(2)}) async-start(), calls=%async_computation.21 | async-start | bytes 42467328 | tf_op jit(solution)/shard_map/reduce_scatter | solution.py:221
  2559.9 2231.8 %reduce-scatter.18.cloned.1.call-start = ((), (), s32[]{:S(2)}) async-start(), calls=%async_computation.22 | async-start | bytes 42467328 | tf_op jit(solution)/shard_map/reduce_scatter | solution.py:222
  2578.3 2309.1 %all-gather.29.cloned.1.call-start = ((), (), s32[]{:S(2)}) async-start(), calls=%async_computation.16 | async-start | bytes 5308416 | tf_op jit(solution)/shard_map/all_gather | solution.py:177
  2578.9 2605.5 %all-reduce.13.cloned.1.call-start = ((), (), s32[]{:S(2)}) async-start(), calls=%async_computation.24 | async-start | bytes 33816576 | tf_op jit(solution)/shard_map/psum | solution.py:293
  4791.8 95.6 %copy-start.13 = (bf16[256,12,128]{0,2,1:T(8,128)(2,1)S(1)}, bf16[256,12,128]{0,2,1:T(8,128)(2,1)}, u32[]{:S(2)}) copy-start(bf16[256,12,128]{0,2,1:T(8,128)(2,1)} %copy-done.12) | copy-start | bytes 2359300
  (46 other events, 393.9 us)
Sparse Core Ops, SparseCore 0:
  10.2 93.6 all-gather.10
  106.0 80.3 all-gather.12
  188.0 362.7 all-gather.14
  552.2 362.4 all-gather.16
  916.0 362.4 all-gather.18
  1321.2 363.6 all-gather.20
  1686.4 362.4 all-gather.22
  2050.5 362.4 all-gather.24
  2415.1 77.6 all-gather.26
  2504.7 63.2 reduce-scatter.9
  2571.9 63.7 reduce-scatter.11
  2639.1 162.5 reduce-scatter.7
  2805.3 162.3 reduce-scatter.13
  2971.4 604.2 reduce-scatter.19
  3579.9 604.1 reduce-scatter.15
  4187.8 603.9 reduce-scatter.17
  4794.1 93.3 all-gather.28
  4890.9 293.3 all-reduce.12
where the time goes:
time: 5220 us; the launch traced here: 5210 us
  waiting for transfers between devices  4680 us (90%)
  blocking collectives  193 us (4%)
  matrix products  187 us (4%)
  local copies, waits for them, and re-layouts  72.5 us (1%)
  other arithmetic  58.7 us (1%)
    reduce_scatter x1, waiting for transfers between devices, shards(): lax.psum_scatter(gate_weight_grad, 'shard', scatter_dimension=1, tiled=True)  608 us
    reduce_scatter x1, waiting for transfers between devices, shards(): lax.psum_scatter(down_weight_grad, 'shard', scatter_dimension=1, tiled=True)  608 us
    reduce_scatter x1, waiting for transfers between devices, shards(): lax.psum_scatter(up_weight_grad, 'shard', scatter_dimension=1, tiled=True)  608 us
    all_gather x1, waiting for transfers between devices, shards(): lax.all_gather(gate_weight, 'shard', axis=1, tiled=True)  354 us
    all_gather x1, waiting for transfers between devices, shards(): lax.all_gather(bound[2], 'shard', axis=1, tiled=True)  351 us
    all_gather x1, waiting for transfers between devices, shards(): lax.all_gather(up_weight, 'shard', axis=1, tiled=True)  350 us
    all_gather x1, waiting for transfers between devices, shards(): lax.all_gather(down_weight, 'shard', axis=1, tiled=True)  348 us
    all_gather x1, waiting for transfers between devices, shards(): lax.all_gather(bound[1], 'shard', axis=1, tiled=True)  347 us
  transfers between devices with their start and end apart: 18, of which 17 were waited for; matrix products, arithmetic and copies ran while one was open for 5% of the time, Pallas kernels for 0%

commit v1 on v0

v1 whole, which is shorter than its diff:
```python
import jax
import jax.numpy as jnp
from jax import lax
from jax.sharding import Mesh
from jax.sharding import PartitionSpec as P

HEADS = 12
KV_HEADS = 2
HEAD_DIM = 128
EXPERTS = 8

epsilon = 1e-06
rotary_base = 1000000.0
masked_score = -1e30

F32 = jnp.float32
BF16 = jnp.bfloat16


def norm_back(values, scale_gain, upstream):
    inverse = lax.rsqrt(jnp.mean(values * values, axis=-1, keepdims=True) + epsilon)
    normal = values * inverse
    gain_grad = jnp.sum(upstream * normal, axis=0)
    scaled = upstream * scale_gain
    value_grad = inverse * (scaled - normal * jnp.mean(scaled * normal, axis=-1, keepdims=True))
    return (value_grad, gain_grad)


def rms_norm(values, scale_gain):
    return (
        values * lax.rsqrt(jnp.mean(values * values, axis=-1, keepdims=True) + epsilon) * scale_gain
    )


def rotary_tables(length, head_width):
    half_width = head_width // 2
    frequency = rotary_base ** (-2.0 * jnp.arange(half_width, dtype=jnp.float32) / head_width)
    angles = jnp.arange(length, dtype=jnp.float32)[:, None] * frequency[None, :]
    return (jnp.cos(angles)[:, None, :], jnp.sin(angles)[:, None, :])


def rotate(values, cosine, sine_table):
    half_width = values.shape[-1] // 2
    first_half = values[..., :half_width]
    second_half = values[..., half_width:]
    return jnp.concatenate(
        [
            first_half * cosine - second_half * sine_table,
            second_half * cosine + first_half * sine_table,
        ],
        axis=-1,
    )


def dot(a, b, dims):
    return lax.dot_general(a, b, (dims, ((), ())), preferred_element_type=F32)


def swap(value, axes):
    count = 2 ** len(axes)
    return lax.ppermute(value, axes, [(i, count - 1 - i) for i in range(count)])


def ordered(mine, other, place):
    first = jnp.where(place == 0, mine, other)
    second = jnp.where(place == 0, other, mine)
    return jnp.stack([first, second])


def line_steps(depth):
    up = [(i, i + 1) for i in range(depth - 1)]
    down = [(i + 1, i) for i in range(depth - 1)]
    return up, down


def line_gather(block, depth, place):
    up, down = line_steps(depth)
    below, above = [], []
    a = b = block
    for _ in range(depth - 1):
        a = lax.ppermute(a, "z", up)
        b = lax.ppermute(b, "z", down)
        below.append(a)
        above.append(b)
    around = jnp.stack(below[::-1] + [block] + above)
    return lax.dynamic_slice_in_dim(around, depth - 1 - place, depth, 0)


def line_scatter(blocks, depth, place):
    up, down = line_steps(depth)

    def at(index):
        return lax.dynamic_index_in_dim(blocks, jnp.clip(index, 0, depth - 1), 0, keepdims=False)

    a = b = None
    for step in range(1, depth):
        send_a = at(depth - step + place)
        send_b = at(place - 1 - (depth - 1) + step - 0)
        if a is not None:
            send_a = (send_a.astype(F32) + a.astype(F32)).astype(BF16)
            send_b = (send_b.astype(F32) + b.astype(F32)).astype(BF16)
        a = lax.ppermute(send_a, "z", up)
        b = lax.ppermute(send_b, "z", down)
    total = at(place).astype(F32)
    if a is not None:
        total = total + a.astype(F32) + b.astype(F32)
    return total


def slab_gather(block):
    by_x = swap(block, ("x",))
    by_y = swap(block, ("y",))
    by_xy = swap(block, ("y", "x"))
    chips = jnp.stack([block, by_y, by_x, by_xy])
    mate = swap(chips, ("c",))
    return jnp.stack([chips, mate], axis=1)


def slab_return(parts):
    mate = swap(parts[:, 1], ("c",))
    both = parts[:, 0].astype(F32) + mate.astype(F32)
    low = both.astype(BF16)
    by_y = swap(low[1], ("y",))
    by_x = swap(low[2], ("x",))
    by_xy = swap(low[3], ("y", "x"))
    return both[0] + by_x.astype(F32) + by_y.astype(F32) + by_xy.astype(F32)


def make_shards(sizes):
    depth = sizes["z"]

    def shards(
        hidden_in,
        segments,
        routes,
        gate_weights,
        grad_out,
        attn_gain,
        query_weight,
        key_weight,
        value_weight,
        output_weight,
        ffn_gain,
        gate_weight,
        up_weight,
        down_weight,
    ):
        length, width = hidden_in.shape
        groups = HEADS // KV_HEADS
        factor = HEAD_DIM ** (-0.5)
        x, y, c, z = (lax.axis_index(n) for n in ("x", "y", "c", "z"))
        expert = 4 * x + 2 * y + c
        mine = 2 * y + c

        gains = jnp.stack([attn_gain, ffn_gain], axis=1)
        gains = jnp.pad(gains, ((0, 0), (0, 126)))
        packed = jnp.concatenate(
            [query_weight, key_weight, value_weight, output_weight, gains], axis=1
        )
        rows, columns = packed.shape
        quarter = rows // 4
        block = lax.dynamic_slice_in_dim(packed, mine * quarter, quarter, 0)
        held = line_gather(block, depth, z)
        held = ordered(held, swap(held, ("x",)), x)
        held = ordered(held, swap(held, ("y",)), y)
        held = ordered(held, swap(held, ("c",)), c)
        held = held.transpose(3, 2, 1, 0, 4, 5).reshape(width, columns)
        qkv = HEADS * HEAD_DIM + 2 * KV_HEADS * HEAD_DIM
        qkv_full = held[:, :qkv]
        output_full = held[:, qkv : qkv + width]
        gain_first = held[:, qkv + width].astype(F32)
        gain_second = held[:, qkv + width + 1].astype(F32)

        def expert_gather(weight):
            own = lax.dynamic_index_in_dim(weight, expert, 0, keepdims=False)
            away = lax.dynamic_index_in_dim(weight, expert ^ 4, 0, keepdims=False)
            pair = ordered(own, swap(away, ("x",)), x)
            full = line_gather(pair, depth, z)
            return full.reshape(-1, full.shape[-1])

        gate_full = expert_gather(gate_weight)
        up_full = expert_gather(up_weight)
        down_full = expert_gather(down_weight)

        onehot = routes[:, :, None] == jnp.arange(EXPERTS, dtype=jnp.int32)
        shares = jnp.sum(jnp.where(onehot, gate_weights[:, :, None], 0.0), axis=1)
        shares = slab_gather(shares).reshape(-1, EXPERTS)
        share = jnp.sum(
            jnp.where(jnp.arange(EXPERTS) == expert, shares, 0.0), axis=1, keepdims=True
        )
        grads = slab_gather(grad_out).reshape(-1, width)

        inputs = hidden_in.astype(F32)
        normed = rms_norm(inputs, gain_first).astype(BF16)
        projected = dot(normed, qkv_full, ((1,), (0,)))
        query_raw = projected[:, : HEADS * HEAD_DIM]
        key_raw = projected[:, HEADS * HEAD_DIM : HEADS * HEAD_DIM + KV_HEADS * HEAD_DIM]
        value_heads = projected[:, HEADS * HEAD_DIM + KV_HEADS * HEAD_DIM :]
        value_heads = value_heads.astype(BF16).reshape(length, KV_HEADS, HEAD_DIM)
        cosine, sine_table = rotary_tables(length, HEAD_DIM)
        rotated_queries = rotate(
            query_raw.reshape(length, HEADS, HEAD_DIM), cosine, sine_table
        ).astype(BF16)
        rotated_keys = rotate(
            key_raw.reshape(length, KV_HEADS, HEAD_DIM), cosine, sine_table
        ).astype(BF16)
        grouped = rotated_queries.reshape(length, KV_HEADS, groups, HEAD_DIM)
        segment = segments[0]
        position = jnp.arange(length, dtype=jnp.int32)
        allowed = (position[:, None] >= position[None, :]) & (segment[:, None] == segment[None, :])
        scores = (
            jnp.einsum("ikgd,jkd->kgij", grouped, rotated_keys, preferred_element_type=F32) * factor
        )
        scores = jnp.where(allowed, scores, masked_score)
        top_score = jnp.max(scores, axis=-1, keepdims=True)
        exponent_terms = jnp.exp(scores - top_score)
        probability = exponent_terms / jnp.sum(exponent_terms, axis=-1, keepdims=True)
        probability_low = probability.astype(BF16)
        attended = jnp.einsum(
            "kgij,jkd->ikgd", probability_low, value_heads, preferred_element_type=F32
        )
        attended = attended.reshape(length, HEADS * HEAD_DIM).astype(BF16)
        mixed = inputs + dot(attended, output_full, ((1,), (0,)))
        normed_two = rms_norm(mixed, gain_second).astype(BF16)

        rows_in = slab_gather(normed_two).reshape(-1, width)
        gate_proj = dot(rows_in, gate_full, ((1,), (0,)))
        up_proj = dot(rows_in, up_full, ((1,), (0,)))
        sigmoid_gate = jax.nn.sigmoid(gate_proj)
        silu_gate = gate_proj * sigmoid_gate
        hidden_act = (silu_gate * up_proj).astype(BF16)
        expert_grad = (share * grads.astype(F32)).astype(BF16)
        down_grad = dot(hidden_act, expert_grad, ((0,), (0,))).astype(BF16)
        expert_out = dot(hidden_act, down_full, ((1,), (0,)))
        expert_part = (share * expert_out).astype(BF16).reshape(4, 2, length, width)
        hidden_grad = dot(expert_grad, down_full, ((1,), (1,)))
        gate_grad = (
            hidden_grad * up_proj * sigmoid_gate * (1.0 + gate_proj * (1.0 - sigmoid_gate))
        ).astype(BF16)
        up_grad = (hidden_grad * silu_gate).astype(BF16)
        rows_grad = dot(gate_grad, gate_full, ((1,), (1,))) + dot(up_grad, up_full, ((1,), (1,)))
        rows_grad = rows_grad.astype(BF16).reshape(4, 2, length, width)
        gate_weight_grad = dot(rows_in, gate_grad, ((0,), (0,))).astype(BF16)
        up_weight_grad = dot(rows_in, up_grad, ((0,), (0,))).astype(BF16)

        layer_out = (mixed + slab_return(expert_part)).astype(BF16)
        normed_two_grad = slab_return(rows_grad)

        def over_outer(value):
            return lax.psum(value, "o") if sizes["o"] > 1 else value

        def expert_scatter(grad):
            shard = grad.shape[0] // (2 * depth)
            blocks = grad.reshape(depth, 2, shard, grad.shape[1])
            total = over_outer(line_scatter(blocks, depth, z)).astype(BF16)
            own = lax.dynamic_index_in_dim(total, x, 0, keepdims=False)
            away = lax.dynamic_index_in_dim(total, 1 - x, 0, keepdims=False)
            four = ordered(own, swap(away, ("x",)), x)[:, None]
            four = ordered(four, swap(four, ("y",)), y)
            four = ordered(four, swap(four, ("c",)), c)
            return four.transpose(2, 1, 0, 3, 4, 5).reshape(EXPERTS, shard, -1).astype(F32)

        total_down = expert_scatter(down_grad)
        total_gate = expert_scatter(gate_weight_grad)
        total_up = expert_scatter(up_weight_grad)

        upstream = grad_out.astype(F32)
        mixed_part, ffn_gain_grad = norm_back(mixed, gain_second, normed_two_grad)
        mixed_grad = upstream + mixed_part
        mixed_low = mixed_grad.astype(BF16)
        output_weight_grad = dot(attended, mixed_low, ((0,), (0,)))
        attended_grad = dot(mixed_low, output_full, ((1,), (1,)))
        attended_grad = attended_grad.astype(BF16).reshape(length, KV_HEADS, groups, HEAD_DIM)
        prob_grad = jnp.einsum(
            "ikgd,jkd->kgij", attended_grad, value_heads, preferred_element_type=F32
        )
        value_grad = jnp.einsum(
            "kgij,ikgd->jkd", probability_low, attended_grad, preferred_element_type=F32
        )
        value_grad = value_grad.astype(BF16).reshape(length, KV_HEADS * HEAD_DIM)
        score_grad = (
            probability * (prob_grad - jnp.sum(probability * prob_grad, axis=-1, keepdims=True))
        ).astype(BF16)
        query_rot_grad = (
            jnp.einsum("kgij,jkd->ikgd", score_grad, rotated_keys, preferred_element_type=F32)
            * factor
        )
        key_rot_grad = (
            jnp.einsum("kgij,ikgd->jkd", score_grad, grouped, preferred_element_type=F32) * factor
        )
        query_raw_grad = rotate(
            query_rot_grad.reshape(length, HEADS, HEAD_DIM), cosine, -sine_table
        )
        query_raw_grad = query_raw_grad.astype(BF16).reshape(length, HEADS * HEAD_DIM)
        key_raw_grad = (
            rotate(key_rot_grad, cosine, -sine_table)
            .astype(BF16)
            .reshape(length, KV_HEADS * HEAD_DIM)
        )
        qkv_grad = jnp.concatenate([query_raw_grad, key_raw_grad, value_grad], axis=1)
        normed_grad = dot(qkv_grad, qkv_full, ((1,), (1,)))
        qkv_weight_grad = dot(normed, qkv_grad, ((0,), (0,)))
        input_part, attn_gain_grad = norm_back(inputs, gain_first, normed_grad)
        grad_in = (mixed_grad + input_part).astype(BF16)

        gain_grads = jnp.stack([attn_gain_grad, ffn_gain_grad], axis=1)
        gain_grads = jnp.pad(gain_grads, ((0, 0), (0, 126)))
        packed_grad = jnp.concatenate(
            [qkv_weight_grad, output_weight_grad, gain_grads], axis=1
        ).astype(BF16)
        parts = packed_grad.reshape(depth, 2, 2, 2, quarter, columns)
        parts = parts.transpose(3, 1, 2, 0, 4, 5)

        def pick(value, place):
            return lax.dynamic_index_in_dim(value, place, 0, keepdims=False)

        def halve(value, axis, place):
            other = swap(pick(value, 1 - place), (axis,))
            return (pick(value, place).astype(F32) + other.astype(F32)).astype(BF16)

        parts = halve(parts, "c", c)
        parts = halve(parts, "x", x)
        parts = halve(parts, "y", y)
        total = over_outer(line_scatter(parts, depth, z)).astype(BF16)
        total = ordered(total, swap(total, ("c",)), c)
        total = ordered(total, swap(total, ("y",)), y).reshape(rows, columns).astype(F32)
        kv = KV_HEADS * HEAD_DIM
        return (
            layer_out,
            grad_in,
            total[:, qkv + width],
            total[:, : qkv - 2 * kv],
            total[:, qkv - 2 * kv : qkv - kv],
            total[:, qkv - kv : qkv],
            total[:, qkv : qkv + width],
            total[:, qkv + width + 1],
            total_gate,
            total_up,
            total_down,
        )

    return shards


def solution(mesh):
    reps, shard_count = mesh.shape["rep"], mesh.shape["shard"]
    sizes = {"o": reps // 4, "y": 2, "c": 2, "z": shard_count // 2, "x": 2}
    fine = Mesh(mesh.devices.reshape(tuple(sizes.values())), tuple(sizes))
    tokens = P(("o", "y", "c", "z", "x"), None)
    first, second = P(("z", "x")), P(None, ("z", "x"), None)
    matrix = P(("z", "x"), None)
    return jax.shard_map(
        make_shards(sizes),
        mesh=fine,
        in_specs=(
            (tokens,) * 5 + (first, matrix, matrix, matrix, matrix, first) + (second,) * 3
        ),
        out_specs=(
            (tokens,) * 2 + (first, matrix, matrix, matrix, matrix, first) + (second,) * 3
        ),
        check_vma=False,
    )
```

time: 5220 us -> 898 us (0.17)
  waiting for transfers between devices: 4680 us -> 387 us
  starting transfers between devices: 0.97 us -> 211 us
  blocking collectives: 193 us -> 0 us
  matrix products: 187 us -> 105 us
    reduce_scatter x7 -> x0, waiting for transfers between devices: 2210 us -> none  [the longest x1 608 us: shards(): lax.psum_scatter(gate_weight_grad, 'shard', scatter_dimension=1, tiled=True)]
    all_gather x10 -> x0, waiting for transfers between devices: 2210 us -> none  [the longest x1 354 us: shards(): lax.all_gather(gate_weight, 'shard', axis=1, tiled=True)]
    ppermute x0 -> x88, waiting for transfers between devices: none -> 387 us  [the longest x40 240 us: swap(): return lax.ppermute(value, axes, [(i, count - 1 - i) for i in range(count)])]
    psum x1 -> x0, waiting for transfers between devices: 248 us -> none  [shards(): lax.psum((share_gain_one, share_query, share_key, share_value, share_outp...]
    ppermute x0 -> x88, starting transfers between devices: none -> 211 us  [the longest x40 82.8 us: swap(): return lax.ppermute(value, axes, [(i, count - 1 - i) for i in range(count)])]
    all_gather x4 -> x0, blocking collectives: 115 us -> none  [the longest x1 29.7 us: shards(): lax.all_gather(key_weight, 'shard', axis=0, tiled=True)]
    dot_general x21 -> x15, matrix products: 174 us -> 92.4 us  [dot(): return lax.dot_general(a, b, (dims, ((), ())), preferred_element_type=F32)]
    unnamed x3 -> x0, blocking collectives: 64.1 us -> none
  transfers between devices with their start and end apart: 18 -> 88, of which waited for: 17 -> 43; matrix products, arithmetic and copies ran while one was open for 5% -> 20% of each run, Pallas kernels for 0% -> 0%
where the time goes in v1:
time: 898 us; the launch traced here: 887 us
  waiting for transfers between devices  387 us (43%)
  starting transfers between devices  211 us (23%)
  matrix products  105 us (12%)
  other arithmetic  103 us (11%)
  local copies, waits for them, and re-layouts  78.3 us (9%)
    ppermute x40, waiting for transfers between devices, swap(): return lax.ppermute(value, axes, [(i, count - 1 - i) for i in range(count)])  240 us
    dot_general x15, matrix products, dot(): return lax.dot_general(a, b, (dims, ((), ())), preferred_element_type=F32)  92.4 us
    ppermute x40, starting transfers between devices, swap(): return lax.ppermute(value, axes, [(i, count - 1 - i) for i in range(count)])  82.8 us
    ppermute x12, waiting for transfers between devices, line_gather(): a = lax.ppermute(a, 'z', up)  76.6 us
    ppermute x12, starting transfers between devices, line_scatter(): a = lax.ppermute(send_a, 'z', up)  39 us
    ppermute x12, starting transfers between devices, line_gather(): a = lax.ppermute(a, 'z', up)  35.8 us
    unnamed x172, local copies, waits for them, and re-layouts  35.1 us
    ppermute x12, waiting for transfers between devices, line_scatter(): b = lax.ppermute(send_b, 'z', down)  35 us
  transfers between devices with their start and end apart: 88, of which 43 were waited for; matrix products, arithmetic and copies ran while one was open for 20% of the time, Pallas kernels for 0%

profile of v1, /device:TPU:13, one launch (start us, length us, event | category | flops | bytes accessed | tf_op | source)
XLA Modules:
  0.0 887.4 jit_solution(10263873189988907865)
XLA Ops:
  42.5 28.0 %collective-permute-done.6 = bf16[4,48,3712]{2,1,0:T(8,128)(2,1)} collective-permute-done((bf16[4,48,3712]{2,1,0:T(8,128)(2,1)S(1)}, bf16[4,48,3712]{2,1,0:T(8,128)(2,1)}, u32[]{:S(2)}, u32[]{:S(2)}) %collective-permute-start.6) | collective-permute-done | bytes 1425440 | tf_op jit(solution)/shard_map/ppermute | solution.py:61
  90.1 60.6 %collective-permute-done.9 = f32[256,8]{0,1:T(8,128)S(1)} collective-permute-done((f32[256,8]{0,1:T(8,128)S(1)}, f32[256,8]{0,1:T(8,128)S(1)}, u32[]{:S(2)}, u32[]{:S(2)}) %collective-permute-start.9) | collective-permute-done | bytes 8224 | tf_op jit(solution)/shard_map/ppermute | solution.py:61
  165.1 8.1 collective-permute-start.12
  181.5 9.9 %collective-permute-done.25 = bf16[2,192,768]{2,1,0:T(8,128)(2,1)} collective-permute-done((bf16[2,192,768]{2,1,0:T(8,128)(2,1)}, bf16[2,192,768]{2,1,0:T(8,128)(2,1)}, u32[]{:S(2)}, u32[]{:S(2)}) %collective-permute-start.25) | collective-permute-done | bytes 589856 | tf_op jit(solution)/shard_map/ppermute | solution.py:81
  207.2 9.4 %collective-permute-done.26 = bf16[2,192,768]{2,1,0:T(8,128)(2,1)} collective-permute-done((bf16[2,192,768]{2,1,0:T(8,128)(2,1)}, bf16[2,192,768]{2,1,0:T(8,128)(2,1)}, u32[]{:S(2)}, u32[]{:S(2)}) %collective-permute-start.26) | collective-permute-done | bytes 589856 | tf_op jit(solution)/shard_map/ppermute | solution.py:81
  231.1 10.7 %collective-permute-done.19 = bf16[2,192,768]{2,1,0:T(8,128)(2,1)S(1)} collective-permute-done((bf16[2,192,768]{2,1,0:T(8,128)(2,1)}, bf16[2,192,768]{2,1,0:T(8,128)(2,1)S(1)}, u32[]{:S(2)}, u32[]{:S(2)}) %collective-permute-start.19) | collective-permute-done | bytes 589856 | tf_op jit(solution)/shard_map/ppermute | solution.py:81
  245.0 9.4 %collective-permute-done.27 = bf16[2,192,768]{2,1,0:T(8,128)(2,1)S(1)} collective-permute-done((bf16[2,192,768]{2,1,0:T(8,128)(2,1)}, bf16[2,192,768]{2,1,0:T(8,128)(2,1)S(1)}, u32[]{:S(2)}, u32[]{:S(2)}) %collective-permute-start.27) | collective-permute-done | bytes 589856 | tf_op jit(solution)/shard_map/ppermute | solution.py:81
  269.1 10.7 %collective-permute-done.20 = bf16[2,192,768]{2,1,0:T(8,128)(2,1)S(1)} collective-permute-done((bf16[2,192,768]{2,1,0:T(8,128)(2,1)S(1)}, bf16[2,192,768]{2,1,0:T(8,128)(2,1)S(1)}, u32[]{:S(2)}, u32[]{:S(2)}) %collective-permute-start.20) | collective-permute-done | bytes 589856 | tf_op jit(solution)/shard_map/ppermute | solution.py:81
  290.1 10.5 %collective-permute-done.22 = bf16[2,192,768]{2,1,0:T(8,128)(2,1)} collective-permute-done((bf16[2,192,768]{2,1,0:T(8,128)(2,1)S(1)}, bf16[2,192,768]{2,1,0:T(8,128)(2,1)}, u32[]{:S(2)}, u32[]{:S(2)}) %collective-permute-start.22) | collective-permute-done | bytes 589856 | tf_op jit(solution)/shard_map/ppermute | solution.py:82
  360.4 16.0 %collective-permute-done.14 = bf16[256,1536]{1,0:T(8,128)(2,1)S(1)} collective-permute-done((bf16[256,1536]{1,0:T(8,128)(2,1)S(1)}, bf16[256,1536]{1,0:T(8,128)(2,1)S(1)}, u32[]{:S(2)}, u32[]{:S(2)}) %collective-permute-start.14) | collective-permute-done | bytes 786464 | tf_op jit(solution)/shard_map/ppermute | solution.py:61
  408.2 12.2 %multiply_convert_fusion.3 = (bf16[2048,768]{1,0:T(8,128)(2,1)}, bf16[2048,768]{1,0:T(8,128)(2,1)}, bf16[2048,768]{1,0:T(8,128)(2,1)}) fusion(f32[2048,768]{1,0:T(8,128)} %fusion.118, f32[2048,768]{1,0:T(8,128)} %fusion.117, bf16[2048,1536]{1,0:T(8,128)(2,1)S(1)} %bitcast.554, bf16[1536,768]{1,0:T(8,128)(2,1)S(1)} %bitcast.583), kind=kOutput, calls=%fused_computation.16 | convolution fusion | flops 4855431168 | bytes 30670848 | tf_op jit(solution)/shard_map/dot_general | solution.py:56
  420.4 10.1 %fusion.119 = f32[2048,1536]{1,0:T(8,128)} fusion(bf16[2048,768]{1,0:T(8,128)(2,1)} %get-tuple-element.21, bf16[1536,768]{1,0:T(8,128)(2,1)S(1)} %bitcast.586), kind=kOutput, calls=%fused_computation.321 | convolution fusion | flops 4831838208 | bytes 18087936 | tf_op jit(solution)/shard_map/dot_general | solution.py:56
  430.6 8.4 add_convert_fusion
  510.6 13.2 %collective-permute-done.41 = bf16[256,1536]{1,0:T(8,128)(2,1)S(1)} collective-permute-done((bf16[256,1536]{1,0:T(8,128)(2,1)}, bf16[256,1536]{1,0:T(8,128)(2,1)S(1)}, u32[]{:S(2)}, u32[]{:S(2)}) %collective-permute-start.41) | collective-permute-done | bytes 786464 | tf_op jit(solution)/shard_map/ppermute | solution.py:61
  523.9 17.1 %collective-permute-done.40 = bf16[256,1536]{1,0:T(8,128)(2,1)S(1)} collective-permute-done((bf16[256,1536]{1,0:T(8,128)(2,1)}, bf16[256,1536]{1,0:T(8,128)(2,1)S(1)}, u32[]{:S(2)}, u32[]{:S(2)}) %collective-permute-start.40) | collective-permute-done | bytes 786464 | tf_op jit(solution)/shard_map/ppermute | solution.py:61
  708.2 9.0 %collective-permute-done.75 = bf16[2,192,768]{2,1,0:T(8,128)(2,1)S(1)} collective-permute-done((bf16[2,192,768]{2,1,0:T(8,128)(2,1)S(1)}, bf16[2,192,768]{2,1,0:T(8,128)(2,1)S(1)}, u32[]{:S(2)}, u32[]{:S(2)}) %collective-permute-start.75) | collective-permute-done | bytes 589856 | tf_op jit(solution)/shard_map/ppermute | solution.py:103
  717.9 11.9 %collective-permute-done.84 = bf16[2,96,1536]{2,1,0:T(8,128)(2,1)S(1)} collective-permute-done((bf16[2,96,1536]{2,1,0:T(8,128)(2,1)S(1)}, bf16[2,96,1536]{2,1,0:T(8,128)(2,1)S(1)}, u32[]{:S(2)}, u32[]{:S(2)}) %collective-permute-start.84) | collective-permute-done | bytes 589856 | tf_op jit(solution)/shard_map/ppermute | solution.py:103
  730.5 25.1 %collective-permute-done.67 = bf16[192,768]{1,0:T(8,128)(2,1)S(1)} collective-permute-done((bf16[192,768]{1,0:T(8,128)(2,1)S(1)}, bf16[192,768]{1,0:T(8,128)(2,1)S(1)}, u32[]{:S(2)}, u32[]{:S(2)}) %collective-permute-start.67) | collective-permute-done | bytes 294944 | tf_op jit(solution)/shard_map/ppermute | solution.py:61
  769.4 9.8 %collective-permute-start.69 = (bf16[2,2,1,192,768]{4,3,0,1,2:T(8,128)(2,1)S(1)}, bf16[2,2,1,192,768]{4,3,0,1,2:T(8,128)(2,1)S(1)}, u32[]{:S(2)}, u32[]{:S(2)}) collective-permute-start(bf16[2,2,1,192,768]{4,3,0,1,2:T(8,128)(2,1)S(1)} %pad_maximum_fusion.8), channel_id=1, source_target_pairs={{0,8},{8,0},{1,9},{9,1},{2,10},{10,2},{3,11},{11,3},{4,12},{12,4},... | collective-permute-start | bytes 3538952 | tf_op jit(solution)/shard_map/ppermute | solution.py:61
  779.4 12.4 %collective-permute-start.78 = (bf16[2,2,1,192,768]{4,3,0,1,2:T(8,128)(2,1)S(1)}, bf16[2,2,1,192,768]{4,3,0,1,2:T(8,128)(2,1)S(1)}, u32[]{:S(2)}, u32[]{:S(2)}) collective-permute-start(bf16[2,2,1,192,768]{4,3,0,1,2:T(8,128)(2,1)S(1)} %pad_maximum_fusion.9), channel_id=1, source_target_pairs={{0,8},{8,0},{1,9},{9,1},{2,10},{10,2},{3,11},{11,3},{4,12},{12,4},... | collective-permute-start | bytes 3538952 | tf_op jit(solution)/shard_map/ppermute | solution.py:61
  791.8 15.2 %collective-permute-done.52 = bf16[4,48,3712]{2,1,0:T(8,128)(2,1)S(1)} collective-permute-done((bf16[4,48,3712]{2,1,0:T(8,128)(2,1)S(1)}, bf16[4,48,3712]{2,1,0:T(8,128)(2,1)S(1)}, u32[]{:S(2)}, u32[]{:S(2)}) %collective-permute-start.52) | collective-permute-done | bytes 1425440 | tf_op jit(solution)/shard_map/ppermute | solution.py:61
  810.0 9.7 %collective-permute-done.86 = bf16[2,1,96,1536]{3,2,0,1:T(8,128)(2,1)S(1)} collective-permute-done((bf16[2,1,96,1536]{3,2,0,1:T(8,128)(2,1)S(1)}, bf16[2,1,96,1536]{3,2,0,1:T(8,128)(2,1)S(1)}, u32[]{:S(2)}, u32[]{:S(2)}) %collective-permute-start.86) | collective-permute-done | bytes 589856 | tf_op jit(solution)/shard_map/ppermute | solution.py:61
  825.6 12.9 %collective-permute-start.87 = (bf16[2,2,1,96,1536]{4,3,0,1,2:T(8,128)(2,1)S(1)}, bf16[2,2,1,96,1536]{4,3,0,1,2:T(8,128)(2,1)S(1)}, u32[]{:S(2)}, u32[]{:S(2)}) collective-permute-start(bf16[2,2,1,96,1536]{4,3,0,1,2:T(8,128)(2,1)S(1)} %pad_maximum_fusion.10), channel_id=1, source_target_pairs={{0,8},{8,0},{1,9},{9,1},{2,10},{10,2},{3,11},{11,3},{4,12},{12,4},... | collective-permute-start | bytes 3538952 | tf_op jit(solution)/shard_map/ppermute | solution.py:61
  874.0 9.3 %collective-permute-done.60 = bf16[2,48,3712]{2,1,0:T(8,128)(2,1)S(1)} collective-permute-done((bf16[2,48,3712]{2,1,0:T(8,128)(2,1)S(1)}, bf16[2,48,3712]{2,1,0:T(8,128)(2,1)S(1)}, u32[]{:S(2)}, u32[]{:S(2)}) %collective-permute-start.60) | collective-permute-done | bytes 712736 | tf_op jit(solution)/shard_map/ppermute | solution.py:61
  (491 shorter events, 534.6 us)
Async XLA Ops:
  74.4 99.8 %collective-permute-start.7 = (bf16[2,4,48,3712]{3,2,0,1:T(8,128)(2,1)}, bf16[2,4,48,3712]{3,2,0,1:T(8,128)(2,1)}, u32[]{:S(2)}, u32[]{:S(2)}) collective-permute-start(bf16[2,4,48,3712]{3,2,0,1:T(8,128)(2,1)} %pad_maximum_fusion.6), channel_id=1, source_target_pairs={{0,16},{16,0},{1,17},{17,1},{2,18},{18,2},{3,19},{19,3},{4,20},{20... | collective-permute-start | bytes 8552456 | tf_op jit(solution)/shard_map/ppermute | solution.py:61
  77.1 73.6 %collective-permute-start.9 = (f32[256,8]{0,1:T(8,128)S(1)}, f32[256,8]{0,1:T(8,128)S(1)}, u32[]{:S(2)}, u32[]{:S(2)}) collective-permute-start(f32[256,8]{0,1:T(8,128)S(1)} %select_reduce_fusion), channel_id=1, source_target_pairs={{0,16},{16,0},{1,17},{17,1},{2,18},{18,2},{3,19},{19,3},{4,20},{20... | collective-permute-start | bytes 24584 | tf_op jit(solution)/shard_map/ppermute | solution.py:61
  78.3 73.6 %collective-permute-start.24 = (bf16[192,768]{1,0:T(8,128)(2,1)S(1)}, bf16[192,768]{1,0:T(8,128)(2,1)}, u32[]{:S(2)}, u32[]{:S(2)}) collective-permute-start(bf16[192,768]{1,0:T(8,128)(2,1)S(1)} %dynamic-slice_bitcast_fusion.15), channel_id=1, source_target_pairs={{0,1},{1,0},{2,3},{3,2},{4,5},{5,4},{6,7},{7,6},{8,9},{9,8},{10,11... | collective-permute-start | bytes 884744 | tf_op jit(solution)/shard_map/ppermute | solution.py:61
  87.6 107.5 %collective-permute-start.44 = (bf16[256,1536]{1,0:T(8,128)(2,1)}, bf16[256,1536]{1,0:T(8,128)(2,1)}, u32[]{:S(2)}, u32[]{:S(2)}) collective-permute-start(bf16[256,1536]{1,0:T(8,128)(2,1)} %param.18), channel_id=1, source_target_pairs={{0,17},{1,16},{16,1},{17,0},{2,19},{3,18},{18,3},{19,2},{4,21},{5,... | collective-permute-start | bytes 2359304 | tf_op jit(solution)/shard_map/ppermute | solution.py:61
  88.9 107.9 %collective-permute-start.43 = (bf16[256,1536]{1,0:T(8,128)(2,1)}, bf16[256,1536]{1,0:T(8,128)(2,1)}, u32[]{:S(2)}, u32[]{:S(2)}) collective-permute-start(bf16[256,1536]{1,0:T(8,128)(2,1)} %param.18), channel_id=1, source_target_pairs={{0,1},{1,0},{2,3},{3,2},{4,5},{5,4},{6,7},{7,6},{8,9},{9,8},{10,11... | collective-permute-start | bytes 2359304 | tf_op jit(solution)/shard_map/ppermute | solution.py:61
  151.9 68.7 %collective-permute-start.42 = (bf16[256,1536]{1,0:T(8,128)(2,1)}, bf16[256,1536]{1,0:T(8,128)(2,1)}, u32[]{:S(2)}, u32[]{:S(2)}) collective-permute-start(bf16[256,1536]{1,0:T(8,128)(2,1)} %param.18), channel_id=1, source_target_pairs={{0,16},{16,0},{1,17},{17,1},{2,18},{18,2},{3,19},{19,3},{4,20},{20... | collective-permute-start | bytes 2359304 | tf_op jit(solution)/shard_map/ppermute | solution.py:61
  195.2 116.7 %collective-permute-start.8 = (bf16[2,2,4,48,3712]{4,3,0,1,2:T(8,128)(2,1)S(1)}, bf16[2,2,4,48,3712]{4,3,0,1,2:T(8,128)(2,1)S(1)}, u32[]{:S(2)}, u32[]{:S(2)}) collective-permute-start(bf16[2,2,4,48,3712]{4,3,0,1,2:T(8,128)(2,1)S(1)} %pad_maximum_fusion.3), channel_id=1, source_target_pairs={{0,8},{8,0},{1,9},{9,1},{2,10},{10,2},{3,11},{11,3},{4,12},{12,4},... | collective-permute-start | bytes 17104904 | tf_op jit(solution)/shard_map/ppermute | solution.py:61
  220.6 39.4 %collective-permute-start.28 = (bf16[2,192,768]{2,1,0:T(8,128)(2,1)}, bf16[2,192,768]{2,1,0:T(8,128)(2,1)S(1)}, u32[]{:S(2)}, u32[]{:S(2)}) collective-permute-start(bf16[2,192,768]{2,1,0:T(8,128)(2,1)} %pad_maximum_fusion.16), channel_id=1, source_target_pairs={{2,0},{4,2},{6,4},{3,1},{5,3},{7,5},{10,8},{12,10},{14,12},{11,9},... | collective-permute-start | bytes 1769480 | tf_op jit(solution)/shard_map/ppermute | solution.py:82
  284.3 102.9 %collective-permute-start.45 = (bf16[4,256,1536]{2,1,0:T(8,128)(2,1)}, bf16[4,256,1536]{2,1,0:T(8,128)(2,1)}, u32[]{:S(2)}, u32[]{:S(2)}) collective-permute-start(bf16[4,256,1536]{2,1,0:T(8,128)(2,1)} %get-tuple-element.35), channel_id=1, source_target_pairs={{0,8},{8,0},{1,9},{9,1},{2,10},{10,2},{3,11},{11,3},{4,12},{12,4},... | collective-permute-start | bytes 9437192 | tf_op jit(solution)/shard_map/ppermute | solution.py:61
  288.0 58.4 %collective-permute-start.36 = (bf16[2,96,1536]{2,1,0:T(8,128)(2,1)}, bf16[2,96,1536]{2,1,0:T(8,128)(2,1)}, u32[]{:S(2)}, u32[]{:S(2)}) collective-permute-start(bf16[2,96,1536]{2,1,0:T(8,128)(2,1)} %collective-permute-done.35), channel_id=1, source_target_pairs={{2,0},{4,2},{6,4},{3,1},{5,3},{7,5},{10,8},{12,10},{14,12},{11,9},... | collective-permute-start | bytes 1769480 | tf_op jit(solution)/shard_map/ppermute | solution.py:82
  300.7 45.9 %collective-permute-start.30 = (bf16[2,192,768]{2,1,0:T(8,128)(2,1)}, bf16[2,192,768]{2,1,0:T(8,128)(2,1)}, u32[]{:S(2)}, u32[]{:S(2)}) collective-permute-start(bf16[2,192,768]{2,1,0:T(8,128)(2,1)} %collective-permute-done.29), channel_id=1, source_target_pairs={{2,0},{4,2},{6,4},{3,1},{5,3},{7,5},{10,8},{12,10},{14,12},{11,9},... | collective-permute-start | bytes 1769480 | tf_op jit(solution)/shard_map/ppermute | solution.py:82
  302.8 46.1 %collective-permute-start.23 = (bf16[2,192,768]{2,1,0:T(8,128)(2,1)}, bf16[2,192,768]{2,1,0:T(8,128)(2,1)}, u32[]{:S(2)}, u32[]{:S(2)}) collective-permute-start(bf16[2,192,768]{2,1,0:T(8,128)(2,1)} %collective-permute-done.22), channel_id=1, source_target_pairs={{2,0},{4,2},{6,4},{3,1},{5,3},{7,5},{10,8},{12,10},{14,12},{11,9},... | collective-permute-start | bytes 1769480 | tf_op jit(solution)/shard_map/ppermute | solution.py:82
  479.9 43.9 %collective-permute-start.41 = (bf16[256,1536]{1,0:T(8,128)(2,1)}, bf16[256,1536]{1,0:T(8,128)(2,1)S(1)}, u32[]{:S(2)}, u32[]{:S(2)}) collective-permute-start(bf16[256,1536]{1,0:T(8,128)(2,1)} %get-tuple-element.37), channel_id=1, source_target_pairs={{0,17},{1,16},{16,1},{17,0},{2,19},{3,18},{18,3},{19,2},{4,21},{5,... | collective-permute-start | bytes 2359304 | tf_op jit(solution)/shard_map/ppermute | solution.py:61
  481.5 59.5 %collective-permute-start.40 = (bf16[256,1536]{1,0:T(8,128)(2,1)}, bf16[256,1536]{1,0:T(8,128)(2,1)S(1)}, u32[]{:S(2)}, u32[]{:S(2)}) collective-permute-start(bf16[256,1536]{1,0:T(8,128)(2,1)} %get-tuple-element.38), channel_id=1, source_target_pairs={{0,16},{16,0},{1,17},{17,1},{2,18},{18,2},{3,19},{19,3},{4,20},{20... | collective-permute-start | bytes 2359304 | tf_op jit(solution)/shard_map/ppermute | solution.py:61
  491.0 50.0 %collective-permute-start.39 = (bf16[256,1536]{1,0:T(8,128)(2,1)}, bf16[256,1536]{1,0:T(8,128)(2,1)}, u32[]{:S(2)}, u32[]{:S(2)}) collective-permute-start(bf16[256,1536]{1,0:T(8,128)(2,1)} %get-tuple-element.36), channel_id=1, source_target_pairs={{0,1},{1,0},{2,3},{3,2},{4,5},{5,4},{6,7},{7,6},{8,9},{9,8},{10,11... | collective-permute-start | bytes 2359304 | tf_op jit(solution)/shard_map/ppermute | solution.py:61
  580.7 100.3 %collective-permute-start.50 = (bf16[2,2,4,48,3712]{4,3,1,0,2:T(8,128)(2,1)}, bf16[2,2,4,48,3712]{4,3,1,0,2:T(8,128)(2,1)}, u32[]{:S(2)}, u32[]{:S(2)}) collective-permute-start(bf16[2,2,4,48,3712]{4,3,1,0,2:T(8,128)(2,1)} %dynamic-slice_bitcast_fusion), channel_id=1, source_target_pairs={{0,8},{8,0},{1,9},{9,1},{2,10},{10,2},{3,11},{11,3},{4,12},{12,4},... | collective-permute-start | bytes 17104904 | tf_op jit(solution)/shard_map/ppermute | solution.py:61
  688.7 74.2 %collective-permute-start.51 = (bf16[2,4,48,3712]{3,2,0,1:T(8,128)(2,1)S(1)}, bf16[2,4,48,3712]{3,2,0,1:T(8,128)(2,1)S(1)}, u32[]{:S(2)}, u32[]{:S(2)}) collective-permute-start(bf16[2,4,48,3712]{3,2,0,1:T(8,128)(2,1)S(1)} %dynamic-slice_bitcast_fusion.1), channel_id=1, source_target_pairs={{0,1},{1,0},{2,3},{3,2},{4,5},{5,4},{6,7},{7,6},{8,9},{9,8},{10,11... | collective-permute-start | bytes 8552456 | tf_op jit(solution)/shard_map/ppermute | solution.py:61
  707.8 47.8 %collective-permute-start.67 = (bf16[192,768]{1,0:T(8,128)(2,1)S(1)}, bf16[192,768]{1,0:T(8,128)(2,1)S(1)}, u32[]{:S(2)}, u32[]{:S(2)}) collective-permute-start(bf16[192,768]{1,0:T(8,128)(2,1)S(1)} %dynamic-slice_bitcast_fusion.13), channel_id=1, source_target_pairs={{0,1},{1,0},{2,3},{3,2},{4,5},{5,4},{6,7},{7,6},{8,9},{9,8},{10,11... | collective-permute-start | bytes 884744 | tf_op jit(solution)/shard_map/ppermute | solution.py:61
  717.5 44.5 %collective-permute-start.76 = (bf16[192,768]{1,0:T(8,128)(2,1)S(1)}, bf16[192,768]{1,0:T(8,128)(2,1)S(1)}, u32[]{:S(2)}, u32[]{:S(2)}) collective-permute-start(bf16[192,768]{1,0:T(8,128)(2,1)S(1)} %dynamic-slice_bitcast_fusion.12), channel_id=1, source_target_pairs={{0,1},{1,0},{2,3},{3,2},{4,5},{5,4},{6,7},{7,6},{8,9},{9,8},{10,11... | collective-permute-start | bytes 884744 | tf_op jit(solution)/shard_map/ppermute | solution.py:61
  730.1 38.2 %collective-permute-start.85 = (bf16[96,1536]{1,0:T(8,128)(2,1)S(1)}, bf16[96,1536]{1,0:T(8,128)(2,1)S(1)}, u32[]{:S(2)}, u32[]{:S(2)}) collective-permute-start(bf16[96,1536]{1,0:T(8,128)(2,1)S(1)} %dynamic-slice_bitcast_fusion.11), channel_id=1, source_target_pairs={{0,1},{1,0},{2,3},{3,2},{4,5},{5,4},{6,7},{7,6},{8,9},{9,8},{10,11... | collective-permute-start | bytes 884744 | tf_op jit(solution)/shard_map/ppermute | solution.py:61
  763.7 43.3 %collective-permute-start.52 = (bf16[4,48,3712]{2,1,0:T(8,128)(2,1)S(1)}, bf16[4,48,3712]{2,1,0:T(8,128)(2,1)S(1)}, u32[]{:S(2)}, u32[]{:S(2)}) collective-permute-start(bf16[4,48,3712]{2,1,0:T(8,128)(2,1)S(1)} %dynamic-slice_bitcast_fusion.2), channel_id=1, source_target_pairs={{0,16},{16,0},{1,17},{17,1},{2,18},{18,2},{3,19},{19,3},{4,20},{20... | collective-permute-start | bytes 4276232 | tf_op jit(solution)/shard_map/ppermute | solution.py:61
  768.4 51.2 %collective-permute-start.86 = (bf16[2,1,96,1536]{3,2,0,1:T(8,128)(2,1)S(1)}, bf16[2,1,96,1536]{3,2,0,1:T(8,128)(2,1)S(1)}, u32[]{:S(2)}, u32[]{:S(2)}) collective-permute-start(bf16[2,1,96,1536]{3,2,0,1:T(8,128)(2,1)S(1)} %maximum_bitcast_fusion.2), channel_id=1, source_target_pairs={{0,16},{16,0},{1,17},{17,1},{2,18},{18,2},{3,19},{19,3},{4,20},{20... | collective-permute-start | bytes 1769480 | tf_op jit(solution)/shard_map/ppermute | solution.py:61
  769.4 95.2 %collective-permute-start.69 = (bf16[2,2,1,192,768]{4,3,0,1,2:T(8,128)(2,1)S(1)}, bf16[2,2,1,192,768]{4,3,0,1,2:T(8,128)(2,1)S(1)}, u32[]{:S(2)}, u32[]{:S(2)}) collective-permute-start(bf16[2,2,1,192,768]{4,3,0,1,2:T(8,128)(2,1)S(1)} %pad_maximum_fusion.8), channel_id=1, source_target_pairs={{0,8},{8,0},{1,9},{9,1},{2,10},{10,2},{3,11},{11,3},{4,12},{12,4},... | collective-permute-start | bytes 3538952 | tf_op jit(solution)/shard_map/ppermute | solution.py:61
  779.4 85.4 %collective-permute-start.78 = (bf16[2,2,1,192,768]{4,3,0,1,2:T(8,128)(2,1)S(1)}, bf16[2,2,1,192,768]{4,3,0,1,2:T(8,128)(2,1)S(1)}, u32[]{:S(2)}, u32[]{:S(2)}) collective-permute-start(bf16[2,2,1,192,768]{4,3,0,1,2:T(8,128)(2,1)S(1)} %pad_maximum_fusion.9), channel_id=1, source_target_pairs={{0,8},{8,0},{1,9},{9,1},{2,10},{10,2},{3,11},{11,3},{4,12},{12,4},... | collective-permute-start | bytes 3538952 | tf_op jit(solution)/shard_map/ppermute | solution.py:61
  (136 other events, 2371.8 us)

commit v2 on v1

--- a/solution.py
+++ b/solution.py
@@ -1,13 +1,19 @@
+import functools
+
 import jax
 import jax.numpy as jnp
 from jax import lax
+from jax.experimental import pallas as pl
+from jax.experimental.pallas import tpu as pltpu
 from jax.sharding import Mesh
 from jax.sharding import PartitionSpec as P
 
 HEADS = 12
 KV_HEADS = 2
+GROUP = HEADS // KV_HEADS
 HEAD_DIM = 128
 EXPERTS = 8
+LANES = 128
 
 epsilon = 1e-06
 rotary_base = 1000000.0
@@ -15,6 +21,479 @@
 
 F32 = jnp.float32
 BF16 = jnp.bfloat16
+MESH = pl.DeviceIdType.MESH
+VMEM_LIMIT = 60 * 2**20
+
+
+def dot(a, b, dims):
+    return lax.dot_general(a, b, (dims, ((), ())), preferred_element_type=F32)
+
+
+def dot_nn(a, b):
+    return dot(a, b, ((1,), (0,)))
+
+
+def dot_nt(a, b):
+    return dot(a, b, ((1,), (1,)))
+
+
+def dot_tn(a, b):
+    return dot(a, b, ((0,), (0,)))
+
+
+def guarded(cond, body):
+    if cond is None:
+        body()
+    else:
+        pl.when(cond)(body)
+
+
+def both(first, second):
+    if first is None:
+        return second
+    if second is None:
+        return first
+    return jnp.logical_and(first, second)
+
+
+class Net:
+    def __init__(self, send_sems, recv_sems, local_sems, core):
+        self.send_sems, self.recv_sems, self.local_sems = send_sems, recv_sems, local_sems
+        self.away = {"c": 1 - core}
+        self.slots, self.sends, self.locals, self.count, self.done = {}, {}, {}, 0, set()
+
+    def slot(self, key):
+        return self.slots.setdefault(key, len(self.slots))
+
+    def send(self, key, src, dst, device, cond=None):
+        recv, index = self.slot(key), self.count
+        self.count += 1
+
+        def build():
+            return pltpu.make_async_remote_copy(
+                src_ref=src(),
+                dst_ref=dst(),
+                send_sem=self.send_sems.at[index],
+                recv_sem=self.recv_sems.at[recv],
+                device_id=device,
+                device_id_type=MESH,
+            )
+
+        guarded(cond, lambda: build().start())
+        self.sends[key] = (cond, build)
+
+    def sent(self, key):
+        cond, build = self.sends.pop(key)
+        guarded(cond, lambda: build().wait_send())
+
+    def arrive(self, key, dst, cond=None):
+        recv = self.slot(key)
+
+        def wait():
+            pltpu.make_async_remote_copy(
+                src_ref=dst(),
+                dst_ref=dst(),
+                send_sem=self.send_sems.at[0],
+                recv_sem=self.recv_sems.at[recv],
+                device_id=self.away,
+                device_id_type=MESH,
+            ).wait_recv()
+
+        guarded(cond, wait)
+
+    def local(self, key, src, dst):
+        index = len(self.locals)
+        copy = pltpu.make_async_copy(src, dst, self.local_sems.at[index])
+        copy.start()
+        self.locals[key] = copy
+
+    def ready(self, key):
+        if key not in self.done:
+            self.done.add(key)
+            self.locals[key].wait()
+
+    def drain(self):
+        for key in list(self.sends):
+            self.sent(key)
+        for key in self.locals:
+            self.ready(key)
+
+
+def greet(depth, coords):
+    x, y, c, z = coords
+    barrier = pltpu.get_barrier_semaphore()
+    for device in ({"y": 1 - y}, {"y": 1 - y, "x": 1 - x}, {"c": 1 - c}):
+        pl.semaphore_signal(barrier, inc=1, device_id=device, device_id_type=MESH)
+    for zi in range(depth):
+        for xi in range(2):
+
+            def tell(zi=zi, xi=xi):
+                pl.semaphore_signal(
+                    barrier,
+                    inc=1,
+                    device_id={"z": jnp.int32(zi), "x": jnp.int32(xi)},
+                    device_id_type=MESH,
+                )
+
+            pl.when(jnp.logical_or(z != zi, x != xi))(tell)
+    pl.semaphore_wait(barrier, 3 + 2 * depth - 1)
+
+
+def along(depth, z):
+    return (
+        ("up", {"z": z + 1}, z + 1 < depth, lambda k: z - k, lambda k: z - k >= 0),
+        ("down", {"z": z - 1}, z > 0, lambda k: z + k, lambda k: z + k < depth),
+    )
+
+
+class SlabGather:
+    def __init__(self, net, name, coords, dst):
+        self.net, self.name, self.dst = net, name, dst
+        x, y, c, _ = coords
+        self.chips = (
+            (1, {"y": 1 - y}),
+            (2, {"x": 1 - x}),
+            (3, {"y": 1 - y, "x": 1 - x}),
+        )
+        self.mate = {"c": 1 - c}
+
+    def put(self, slot, src, device):
+        self.net.send(
+            (self.name, slot), lambda: src, lambda: self.dst.at[slot], device
+        )
+
+    def start(self, src):
+        for chip, device in self.chips:
+            self.put(2 * chip, src, device)
+        self.put(1, src, self.mate)
+        self.net.local((self.name, "own"), src, self.dst.at[0])
+
+    def forward(self):
+        for chip, _ in self.chips:
+            self.net.arrive((self.name, 2 * chip), lambda: self.dst.at[2 * chip])
+            self.put(2 * chip + 1, self.dst.at[2 * chip], self.mate)
+
+    def finish(self):
+        self.net.ready((self.name, "own"))
+        for slot in (1, 3, 5, 7):
+            self.net.arrive((self.name, slot), lambda: self.dst.at[slot])
+
+
+class AttentionGather:
+    def __init__(self, net, name, depth, coords, src, dst):
+        self.net, self.name, self.depth, self.coords, self.src, self.dst = (
+            net, name, depth, coords, src, dst,
+        )
+        self.rows, self.columns = src.shape[0], src.shape[1] // 4
+
+    def lanes(self, yi, ci):
+        return pl.ds(pl.multiple_of((2 * yi + ci) * self.columns, LANES), self.columns)
+
+    def block(self, zi, xi, yi, ci):
+        rows = pl.ds(pl.multiple_of((zi * 2 + xi) * self.rows, self.rows), self.rows)
+        return lambda: self.dst.at[rows, self.lanes(yi, ci)]
+
+    def put(self, key, place, device, cond=None, src=None):
+        block = self.block(*place)
+        self.net.send((self.name,) + key, src or block, block, device, cond)
+
+    def wait(self, key, place, cond=None):
+        self.net.arrive((self.name,) + key, self.block(*place), cond)
+
+    def start(self):
+        x, y, c, z = self.coords
+        own = lambda: self.src.at[:, self.lanes(y, c)]
+        cross = lambda: self.src.at[:, self.lanes(1 - y, c)]
+        for tag, device, more, _, _ in along(self.depth, z):
+            self.put(("z", tag, 1), (z, x, y, c), device, more, own)
+        self.put(("x", "same"), (z, x, y, c), {"x": 1 - x}, None, own)
+        self.put(("x", "cross"), (z, x, 1 - y, c), {"x": 1 - x}, None, cross)
+        rows = pl.ds(pl.multiple_of((z * 2 + x) * self.rows, self.rows), self.rows)
+        self.net.local((self.name, "own"), self.src, self.dst.at[rows, :])
+
+    def pass_z(self, k):
+        x, y, c, z = self.coords
+        for tag, device, more, origin, there in along(self.depth, z):
+            place, cond = (origin(k), x, y, c), there(k)
+            self.wait(("z", tag, k), place, cond)
+            if k + 1 < self.depth:
+                self.put(("z", tag, k + 1), place, device, both(cond, more))
+            self.put(("x", tag, k), place, {"x": 1 - x}, cond)
+            self.put(("y", tag, k, 0), place, {"y": 1 - y}, cond)
+            self.put(("c", tag, k, 0), place, {"c": 1 - c}, cond)
+
+    def pass_x(self, k):
+        x, y, c, z = self.coords
+        if k == 0:
+            for tag, yi in (("same", y), ("cross", 1 - y)):
+                place = (z, 1 - x, yi, c)
+                self.wait(("x", tag), place)
+                self.put(("c", tag), place, {"c": 1 - c})
+            return
+        for tag, _, _, origin, there in along(self.depth, z):
+            place, cond = (origin(k), 1 - x, y, c), there(k)
+            self.wait(("x", tag, k), place, cond)
+            self.put(("y", tag, k, 1), place, {"y": 1 - y}, cond)
+            self.put(("c", tag, k, 1), place, {"c": 1 - c}, cond)
+
+    def pass_y(self, k):
+        x, y, c, z = self.coords
+        for tag, _, _, origin, there in along(self.depth, z):
+            cond = there(k)
+            for j, xi in ((0, x), (1, 1 - x)):
+                place = (origin(k), xi, 1 - y, c)
+                self.wait(("y", tag, k, j), place, cond)
+                self.put(("c", tag, k, 2 + j), place, {"c": 1 - c}, cond)
+
+    def finish(self):
+        x, y, c, z = self.coords
+        self.net.ready((self.name, "own"))
+        for tag, yi in (("same", y), ("cross", 1 - y)):
+            self.wait(("c", tag), (z, 1 - x, yi, 1 - c))
+        for k in range(1, self.depth):
+            for tag, _, _, origin, there in along(self.depth, z):
+                for j, (xi, yi) in enumerate(((x, y), (1 - x, y), (x, 1 - y), (1 - x, 1 - y))):
+                    self.wait(("c", tag, k, j), (origin(k), xi, yi, 1 - c), there(k))
+
+
+class ExpertGather:
+    def __init__(self, net, name, depth, coords, src, dst):
+        self.net, self.name, self.depth, self.coords, self.src, self.dst = (
+            net, name, depth, coords, src, dst,
+        )
+        self.rows = src.shape[1]
+
+    def block(self, zi, xi):
+        rows = pl.ds(pl.multiple_of((zi * 2 + xi) * self.rows, self.rows), self.rows)
+        return lambda: self.dst.at[rows, :]
+
+    def put(self, key, place, device, cond=None, src=None):
+        block = self.block(*place)
+        self.net.send((self.name,) + key, src or block, block, device, cond)
+
+    def start(self):
+        x, y, c, z = self.coords
+        own = self.src.at[4 * x + 2 * y + c]
+        for tag, device, more, _, _ in along(self.depth, z):
+            self.put(("z", tag, 1, 0), (z, x), device, more, lambda: own)
+        away = self.src.at[4 * (1 - x) + 2 * y + c]
+        self.put(("x",), (z, x), {"x": 1 - x}, None, lambda: away)
+        self.net.local((self.name, "own"), own, self.block(z, x)())
+
+    def pass_x(self):
+        x, y, c, z = self.coords
+        self.net.arrive((self.name, "x"), self.block(z, 1 - x))
+        for tag, device, more, _, _ in along(self.depth, z):
+            self.put(("z", tag, 1, 1), (z, 1 - x), device, more)
+
+    def pass_z(self, k):
+        x, y, c, z = self.coords
+        for j, xi in ((0, x), (1, 1 - x)):
+            for tag, device, more, origin, there in along(self.depth, z):
+                place, cond = (origin(k), xi), there(k)
+                self.net.arrive((self.name, "z", tag, k, j), self.block(*place), cond)
+                if k + 1 < self.depth:
+                    self.put(("z", tag, k + 1, j), place, device, both(cond, more))
+
+    def finish(self):
+        self.net.ready((self.name, "own"))
+
+
+def inverse_rms(values):
+    return lax.rsqrt(jnp.mean(values * values, axis=-1, keepdims=True) + epsilon)
+
+
+def turn(values, cosine, sine):
+    return values * cosine + pltpu.roll(values, HEAD_DIM // 2, axis=1) * sine
+
+
+def forward_kernel(depth, shard_rows, *refs):
+    (
+        hidden, mask, cosine, sine, gains_in, wq_in, wo_in, gate_in, up_in, down_in, grad_in, share_in,
+        wq, wo, gains, gate, up, down, rows, grads, shares,
+        queries, keys, values, probability, attended, mixed, gain_rows,
+        wq_here, wo_here, normed_two, gains_here, send_sems, recv_sems, local_sems,
+    ) = refs
+    coords = x, y, c, z = tuple(lax.axis_index(n) for n in ("x", "y", "c", "z"))
+    net = Net(send_sems, recv_sems, local_sems, c)
+    greet(depth, coords)
+
+    attn = [
+        AttentionGather(net, "wq", depth, coords, wq_in, wq),
+        AttentionGather(net, "wo", depth, coords, wo_in, wo),
+    ]
+    gate_up = [
+        ExpertGather(net, "gate", depth, coords, gate_in, gate),
+        ExpertGather(net, "up", depth, coords, up_in, up),
+    ]
+    down_one = ExpertGather(net, "down", depth, coords, down_in, down)
+
+    me = z * 2 + x
+    base = [net.slot(("gains", s)) for s in range(2 * depth)][0]
+    net.local("gains", gains_in, gains.at[me])
+
+    def gain_copy(s, index):
+        return pltpu.make_async_remote_copy(
+            src_ref=gains_in,
+            dst_ref=gains.at[me],
+            send_sem=send_sems.at[index],
+            recv_sem=recv_sems.at[base + me],
+            device_id={"z": jnp.int32(s // 2), "x": jnp.int32(s % 2)},
+            device_id_type=MESH,
+        )
+
+    gain_sends = []
+    for s in range(2 * depth):
+        index = net.count
+        net.count += 1
+        gain_sends.append((s, index))
+        pl.when(me != s)(lambda: gain_copy(s, index).start())
+
+    for one in attn:
+        one.start()
+    for one in gate_up:
+        one.start()
+    for k in range(1, depth):
+        for one in attn:
+            one.pass_z(k)
+    attn[0].pass_x(0)
+    attn[1].pass_x(0)
+    for k in range(1, depth):
+        for one in attn:
+            one.pass_x(k)
+    for one in gate_up:
+        one.pass_x()
+    share_net = SlabGather(net, "share", coords, shares)
+    share_net.start(share_in)
+    grad_net = SlabGather(net, "grad", coords, grads)
+    grad_net.start(grad_in)
+    for k in range(1, depth):
+        for one in attn:
+            one.pass_y(k)
+    for one in gate_up:
+        one.pass_z(1)
+    down_one.start()
+    attn[0].finish()
+    net.local("wq here", wq, wq_here)
+    for s in range(2 * depth):
+        pl.when(me != s)(
+            lambda: net.arrive(("gains", s), lambda: gains.at[s])
+        )
+    net.ready("gains")
+
+    net.local("gains here", gains, gains_here)
+    net.ready("gains here")
+    wide = None
+    for s in range(2 * depth):
+        rest = jnp.zeros((8, hidden.shape[1] - gains.shape[2]), F32)
+        piece = jnp.concatenate([gains_here[s], rest], axis=1)
+        piece = piece if s == 0 else pltpu.roll(piece, s * shard_rows, axis=1)
+        wide = piece if wide is None else wide + piece
+    gain_rows[...] = wide
+
+    inputs = hidden[...].astype(F32)
+    normed = (inputs * inverse_rms(inputs) * gain_rows[0:1, :]).astype(BF16)
+    cos, sin = cosine[...], sine[...]
+    net.ready("wq here")
+    step = 512
+    length = hidden.shape[0]
+    for start in range(0, wq.shape[1], step):
+        part = dot_nn(normed, wq_here[:, start : start + step])
+        for at in range(start, start + step, HEAD_DIM):
+            head, one = at // HEAD_DIM, part[:, at - start : at - start + HEAD_DIM]
+            if head < HEADS:
+                queries[head * length : (head + 1) * length, :] = turn(one, cos, sin).astype(BF16)
+            elif head < HEADS + KV_HEADS:
+                at_row = (head - HEADS) * length
+                keys[at_row : at_row + length, :] = turn(one, cos, sin).astype(BF16)
+            else:
+                at_row = (head - HEADS - KV_HEADS) * length
+                values[at_row : at_row + length, :] = one.astype(BF16)
+    share_net.forward()
+    grad_net.forward()
+    for one in gate_up:
+        for k in range(2, depth):
+            one.pass_z(k)
+    down_one.pass_x()
+    attn[1].finish()
+    net.local("wo here", wo, wo_here)
+    factor = HEAD_DIM ** (-0.5)
+    allowed = mask[...] > 0.0
+    for head in range(HEADS):
+        kv = head // GROUP
+        here = slice(head * length, (head + 1) * length)
+        there = slice(kv * length, (kv + 1) * length)
+        scores = dot_nt(queries[here, :], keys[there, :]) * factor
+        scores = jnp.where(allowed, scores, masked_score)
+        terms = jnp.exp(scores - jnp.max(scores, axis=-1, keepdims=True))
+        chance = terms / jnp.sum(terms, axis=-1, keepdims=True)
+        probability[here, :] = chance
+        attended[:, head * HEAD_DIM : (head + 1) * HEAD_DIM] = dot_nn(
+            chance.astype(BF16), values[there, :]
+        ).astype(BF16)
+    net.ready("wo here")
+    for start in range(0, wo.shape[1], step):
+        there = slice(start, start + step)
+        mixed[:, there] = hidden[:, there].astype(F32) + dot_nn(attended[...], wo_here[:, there])
+    total = mixed[...]
+    normed_two[...] = (total * inverse_rms(total) * gain_rows[1:2, :]).astype(BF16)
+    row_net = SlabGather(net, "rows", coords, rows)
+    row_net.start(normed_two)
+    down_one.pass_z(1)
+    row_net.forward()
+    for k in range(2, depth):
+        down_one.pass_z(k)
+    share_net.finish()
+    grad_net.finish()
+    row_net.finish()
+    for one in gate_up + [down_one]:
+        one.finish()
+    for s, index in gain_sends:
+        pl.when(me != s)(lambda: gain_copy(s, index).wait_send())
+    net.drain()
+    assert net.count <= send_sems.shape[0] and len(net.slots) <= recv_sems.shape[0]
+
+
+def forward_call(depth, shard_rows, *args):
+    hidden, mask, cosine, sine, gains_in, wq_in, wo_in, gate_in, up_in, down_in, grad_in, share_in = args
+    length, width = hidden.shape
+    shards = 2 * depth
+    here, there = pl.BlockSpec(memory_space=pltpu.VMEM), pl.BlockSpec(memory_space=pltpu.HBM)
+
+    def shape(*dims, dtype=BF16):
+        return jax.ShapeDtypeStruct(dims, dtype)
+
+    wide = wq_in.shape[1]
+    out_shape = [
+        shape(width, wide), shape(width, width), shape(shards, *gains_in.shape, dtype=F32),
+        shape(shards * gate_in.shape[1], gate_in.shape[2]),
+        shape(shards * up_in.shape[1], up_in.shape[2]),
+        shape(shards * down_in.shape[1], down_in.shape[2]),
+        shape(EXPERTS, length, width), shape(EXPERTS, length, width),
+        shape(EXPERTS, length, LANES, dtype=F32),
+        shape(HEADS * length, HEAD_DIM), shape(KV_HEADS * length, HEAD_DIM),
+        shape(KV_HEADS * length, HEAD_DIM), shape(HEADS * length, length, dtype=F32),
+        shape(length, width), shape(length, width, dtype=F32), shape(8, width, dtype=F32),
+    ]
+    sends = 24 * depth * 2 + 80
+    return pl.pallas_call(
+        functools.partial(forward_kernel, depth, shard_rows),
+        out_shape=out_shape,
+        in_specs=[here] * 4 + [there] * 8,
+        out_specs=[there] * 9 + [here] * 7,
+        scratch_shapes=[
+            pltpu.VMEM((width, wide), BF16),
+            pltpu.VMEM((width, width), BF16),
+            pltpu.VMEM((length, width), BF16),
+            pltpu.VMEM((shards, *gains_in.shape), F32),
+            pltpu.SemaphoreType.DMA((sends,)),
+            pltpu.SemaphoreType.DMA((sends,)),
+            pltpu.SemaphoreType.DMA((16,)),
+        ],
+        compiler_params=pltpu.CompilerParams(
+            collective_id=1, has_side_effects=True, vmem_limit_bytes=VMEM_LIMIT
+        ),
+    )(*args)
 
 
 def norm_back(values, scale_gain, upstream):
@@ -50,10 +529,6 @@
         ],
         axis=-1,
     )
-
-
-def dot(a, b, dims):
-    return lax.dot_general(a, b, (dims, ((), ())), preferred_element_type=F32)
 
 
 def swap(value, axes):
@@ -150,80 +625,44 @@
         factor = HEAD_DIM ** (-0.5)
         x, y, c, z = (lax.axis_index(n) for n in ("x", "y", "c", "z"))
         expert = 4 * x + 2 * y + c
-        mine = 2 * y + c
-
-        gains = jnp.stack([attn_gain, ffn_gain], axis=1)
-        gains = jnp.pad(gains, ((0, 0), (0, 126)))
-        packed = jnp.concatenate(
-            [query_weight, key_weight, value_weight, output_weight, gains], axis=1
-        )
-        rows, columns = packed.shape
-        quarter = rows // 4
-        block = lax.dynamic_slice_in_dim(packed, mine * quarter, quarter, 0)
-        held = line_gather(block, depth, z)
-        held = ordered(held, swap(held, ("x",)), x)
-        held = ordered(held, swap(held, ("y",)), y)
-        held = ordered(held, swap(held, ("c",)), c)
-        held = held.transpose(3, 2, 1, 0, 4, 5).reshape(width, columns)
-        qkv = HEADS * HEAD_DIM + 2 * KV_HEADS * HEAD_DIM
-        qkv_full = held[:, :qkv]
-        output_full = held[:, qkv : qkv + width]
-        gain_first = held[:, qkv + width].astype(F32)
-        gain_second = held[:, qkv + width + 1].astype(F32)
-
-        def expert_gather(weight):
-            own = lax.dynamic_index_in_dim(weight, expert, 0, keepdims=False)
-            away = lax.dynamic_index_in_dim(weight, expert ^ 4, 0, keepdims=False)
-            pair = ordered(own, swap(away, ("x",)), x)
-            full = line_gather(pair, depth, z)
-            return full.reshape(-1, full.shape[-1])
-
-        gate_full = expert_gather(gate_weight)
-        up_full = expert_gather(up_weight)
-        down_full = expert_gather(down_weight)
-
-        onehot = routes[:, :, None] == jnp.arange(EXPERTS, dtype=jnp.int32)
+        gains = jnp.stack([attn_gain, ffn_gain]).astype(F32)
+        shard_rows = gains.shape[1]
+        lanes = -(-shard_rows // LANES) * LANES
+        gains = jnp.pad(gains, ((0, 6), (0, lanes - shard_rows)))
+        wq_in = jnp.concatenate([query_weight, key_weight, value_weight], axis=1)
+        onehot = routes[:, :, None] == jnp.arange(LANES, dtype=jnp.int32)
         shares = jnp.sum(jnp.where(onehot, gate_weights[:, :, None], 0.0), axis=1)
-        shares = slab_gather(shares).reshape(-1, EXPERTS)
-        share = jnp.sum(
-            jnp.where(jnp.arange(EXPERTS) == expert, shares, 0.0), axis=1, keepdims=True
-        )
-        grads = slab_gather(grad_out).reshape(-1, width)
-
-        inputs = hidden_in.astype(F32)
-        normed = rms_norm(inputs, gain_first).astype(BF16)
-        projected = dot(normed, qkv_full, ((1,), (0,)))
-        query_raw = projected[:, : HEADS * HEAD_DIM]
-        key_raw = projected[:, HEADS * HEAD_DIM : HEADS * HEAD_DIM + KV_HEADS * HEAD_DIM]
-        value_heads = projected[:, HEADS * HEAD_DIM + KV_HEADS * HEAD_DIM :]
-        value_heads = value_heads.astype(BF16).reshape(length, KV_HEADS, HEAD_DIM)
-        cosine, sine_table = rotary_tables(length, HEAD_DIM)
-        rotated_queries = rotate(
-            query_raw.reshape(length, HEADS, HEAD_DIM), cosine, sine_table
-        ).astype(BF16)
-        rotated_keys = rotate(
-            key_raw.reshape(length, KV_HEADS, HEAD_DIM), cosine, sine_table
-        ).astype(BF16)
-        grouped = rotated_queries.reshape(length, KV_HEADS, groups, HEAD_DIM)
         segment = segments[0]
         position = jnp.arange(length, dtype=jnp.int32)
         allowed = (position[:, None] >= position[None, :]) & (segment[:, None] == segment[None, :])
-        scores = (
-            jnp.einsum("ikgd,jkd->kgij", grouped, rotated_keys, preferred_element_type=F32) * factor
-        )
-        scores = jnp.where(allowed, scores, masked_score)
-        top_score = jnp.max(scores, axis=-1, keepdims=True)
-        exponent_terms = jnp.exp(scores - top_score)
-        probability = exponent_terms / jnp.sum(exponent_terms, axis=-1, keepdims=True)
+        cosine, sine_table = rotary_tables(length, HEAD_DIM)
+        cos_wide = jnp.concatenate([cosine[:, 0], cosine[:, 0]], axis=1)
+        sin_wide = jnp.concatenate([-sine_table[:, 0], sine_table[:, 0]], axis=1)
+        (
+            qkv_full, output_full, _, gate_full, up_full, down_full, rows_in, grads, shares,
+            queries, keys, value_rows, probability, attended, mixed, gain_rows,
+        ) = forward_call(
+            depth, shard_rows, hidden_in, allowed.astype(F32), cos_wide, sin_wide, gains,
+            wq_in, output_weight, gate_weight, up_weight, down_weight, grad_out, shares,
+        )
+        gain_first, gain_second = gain_rows[0], gain_rows[1]
+        share = jnp.sum(
+            jnp.where(jnp.arange(LANES) == expert, shares, 0.0), axis=2
+        ).reshape(-1, 1)
+        rows_in, grads = rows_in.reshape(-1, width), grads.reshape(-1, width)
+        inputs = hidden_in.astype(F32)
+        normed = rms_norm(inputs, gain_first).astype(BF16)
+        probability = probability.reshape(KV_HEADS, groups, length, length)
         probability_low = probability.astype(BF16)
-        attended = jnp.einsum(
-            "kgij,jkd->ikgd", probability_low, value_heads, preferred_element_type=F32
-        )
-        attended = attended.reshape(length, HEADS * HEAD_DIM).astype(BF16)
-        mixed = inputs + dot(attended, output_full, ((1,), (0,)))
-        normed_two = rms_norm(mixed, gain_second).astype(BF16)
-
-        rows_in = slab_gather(normed_two).reshape(-1, width)
+        grouped = queries.reshape(KV_HEADS, groups, length, HEAD_DIM).transpose(2, 0, 1, 3)
+        rotated_keys = keys.reshape(KV_HEADS, length, HEAD_DIM).transpose(1, 0, 2)
+        value_heads = value_rows.reshape(KV_HEADS, length, HEAD_DIM).transpose(1, 0, 2)
+        mine = 2 * y + c
+        rows = shard_rows
+        quarter = rows // 4
+        qkv = wq_in.shape[1]
+        columns = qkv + width + 128
+
         gate_proj = dot(rows_in, gate_full, ((1,), (0,)))
         up_proj = dot(rows_in, up_full, ((1,), (0,)))
         sigmoid_gate = jax.nn.sigmoid(gate_proj)

time: 898 us -> 684 us (0.76)
  waiting for transfers between devices: 387 us -> 168 us
  Pallas kernels: 0 us -> 164 us
  starting transfers between devices: 211 us -> 141 us
  local copies, waits for them, and re-layouts: 78.3 us -> 36.2 us
  other arithmetic: 103 us -> 64.6 us
    pallas_call x0 -> x1, Pallas kernels: none -> 164 us  [forward_call(): pl.pallas_call(functools.partial(forward_kernel, depth, shard_rows), out_...]
    ppermute x40 -> x22, waiting for transfers between devices: 240 us -> 120 us  [swap(): return lax.ppermute(value, axes, [(i, count - 1 - i) for i in range(count)])]
    ppermute x24 -> x0, waiting for transfers between devices: 92.6 us -> none  [the longest x12 76.6 us: line_gather(): a = lax.ppermute(a, 'z', up)]
    ppermute x24 -> x0, starting transfers between devices: 60.9 us -> none  [the longest x12 35.8 us: line_gather(): a = lax.ppermute(a, 'z', up)]
    unnamed x172 -> x88, local copies, waits for them, and re-layouts: 35.1 us -> 9.3 us
    ppermute x40 -> x22, starting transfers between devices: 82.8 us -> 64.3 us  [swap(): return lax.ppermute(value, axes, [(i, count - 1 - i) for i in range(count)])]
    convert_element_type x3 -> x1, other arithmetic: 19.6 us -> 4.01 us  [shards(): expert_grad = (share * grads.astype(F32)).astype(BF16)]
    another operation x28 -> x16, other arithmetic: 15.6 us -> 1.63 us  [ordered(): return jnp.stack([first, second])]
  transfers between devices with their start and end apart: 88 -> 46, of which waited for: 43 -> 21; matrix products, arithmetic and copies ran while one was open for 20% -> 14% of each run, Pallas kernels for 0% -> 0%
where the time goes in v2:
time: 684 us; the launch traced here: 674 us
  waiting for transfers between devices  168 us (25%)
  Pallas kernels  164 us (24%)
  starting transfers between devices  141 us (21%)
  matrix products  97 us (14%)
  other arithmetic  64.6 us (9%)
  local copies, waits for them, and re-layouts  36.2 us (5%)
    pallas_call x1, Pallas kernels, forward_call(): pl.pallas_call(functools.partial(forward_kernel, depth, shard_rows), out_...  164 us
    ppermute x22, waiting for transfers between devices, swap(): return lax.ppermute(value, axes, [(i, count - 1 - i) for i in range(count)])  120 us
    dot_general x13, matrix products, dot(): return lax.dot_general(a, b, (dims, ((), ())), preferred_element_type=F32)  92.8 us
    ppermute x22, starting transfers between devices, swap(): return lax.ppermute(value, axes, [(i, count - 1 - i) for i in range(count)])  64.3 us
    ppermute x12, starting transfers between devices, line_scatter(): b = lax.ppermute(send_b, 'z', down)  39.9 us
    ppermute x12, starting transfers between devices, line_scatter(): a = lax.ppermute(send_a, 'z', up)  37.3 us
    ppermute x12, waiting for transfers between devices, line_scatter(): b = lax.ppermute(send_b, 'z', down)  29.4 us
    ppermute x12, waiting for transfers between devices, line_scatter(): a = lax.ppermute(send_a, 'z', up)  19 us
  transfers between devices with their start and end apart: 46, of which 21 were waited for; matrix products, arithmetic and copies ran while one was open for 14% of the time, Pallas kernels for 0%

profile of v2, /device:TPU:13, one launch (start us, length us, event | category | flops | bytes accessed | tf_op | source)
XLA Modules:
  0.0 673.6 jit_solution(15395398671178081213)
XLA Ops:
  9.3 164.2 %shard_map.221 = (bf16[1536,2048]{1,0:T(8,128)(2,1)}, bf16[1536,1536]{1,0:T(8,128)(2,1)}, f32[8,8,256]{2,1,0:T(8,128)}, bf16[1536,768]{1,0:T(8,128)(2,1)}, bf16[...) custom-call(bf16[256,1536]{1,0:T(8,128)(2,1)} %refs_0_.1, ...), custom_call_target="tpu_custom_call" | custom-call | tf_op jit(solution)/shard_map/pallas_call | solution.py:479
  173.6 9.9 %fusion.95 = f32[2048,768]{1,0:T(8,128)} fusion(bf16[2048,1536]{1,0:T(8,128)(2,1)} %bitcast.408, bf16[1536,768]{1,0:T(8,128)(2,1)} %get-tuple-element.29), kind=kOutput, calls=%fused_computation.226 | convolution fusion | flops 4831838208 | bytes 14942208 | tf_op jit(solution)/shard_map/dot_general | solution.py:29
  183.5 7.0 %fusion.96 = f32[2048,768]{1,0:T(8,128)} fusion(bf16[2048,1536]{1,0:T(8,128)(2,1)S(1)} %bitcast.410, bf16[1536,768]{1,0:T(8,128)(2,1)S(1)} %copy-done.29), kind=kOutput, calls=%fused_computation.227 | convolution fusion | flops 4831838208 | bytes 14942208 | tf_op jit(solution)/shard_map/dot_general | solution.py:29
  194.9 14.0 %multiply_convert_fusion.1 = (bf16[2048,768]{1,0:T(8,128)(2,1)S(1)}, bf16[2048,768]{1,0:T(8,128)(2,1)}, bf16[2048,768]{1,0:T(8,128)(2,1)}) fusion(f32[2048,768]{1,0:T(8,128)} %fusion.95, f32[2048,768]{1,0:T(8,128)} %fusion.96, bf16[2048,1536]{1,0:T(8,128)(2,1)S(1)} %fusion, bf16[768,1536]{1,0:T(8,128)(2,1)S(1)} %copy-done.28), kind=kOutput, calls=%fused_computation.11 | convolution fusion | flops 4855431168 | bytes 30670848 | tf_op jit(solution)/shard_map/dot_general | solution.py:29
  208.9 11.1 %fusion.97 = f32[2048,1536]{1,0:T(8,128)} fusion(bf16[2048,768]{1,0:T(8,128)(2,1)} %get-tuple-element.51, bf16[1536,768]{1,0:T(8,128)(2,1)S(1)} %copy-done.31), kind=kOutput, calls=%fused_computation.228 | convolution fusion | flops 4831838208 | bytes 18087936 | tf_op jit(solution)/shard_map/dot_general | solution.py:29
  220.0 8.8 %add_convert_fusion = bf16[2048,1536]{1,0:T(8,128)(2,1)S(1)} fusion(f32[2048,1536]{1,0:T(8,128)} %fusion.97, bf16[2048,768]{1,0:T(8,128)(2,1)S(1)} %get-tuple-element.50, bf16[1536,768]{1,0:T(8,128)(2,1)S(1)} %copy-done.30), kind=kOutput, calls=%fused_computation.2 | convolution fusion | flops 4838129664 | bytes 24379392 | tf_op jit(solution)/shard_map/dot_general | solution.py:29
  253.9 9.4 %collective-permute-done.7 = bf16[256,1536]{1,0:T(8,128)(2,1)S(1)} collective-permute-done((bf16[256,1536]{1,0:T(8,128)(2,1)S(1)}, bf16[256,1536]{1,0:T(8,128)(2,1)S(1)}, u32[]{:S(2)}, u32[]{:S(2)}) %collective-permute-start.7) | collective-permute-done | bytes 786464 | tf_op jit(solution)/shard_map/ppermute | solution.py:536
  270.0 13.1 %collective-permute-done.6 = bf16[256,1536]{1,0:T(8,128)(2,1)} collective-permute-done((bf16[256,1536]{1,0:T(8,128)(2,1)}, bf16[256,1536]{1,0:T(8,128)(2,1)}, u32[]{:S(2)}, u32[]{:S(2)}) %collective-permute-start.6) | collective-permute-done | bytes 786464 | tf_op jit(solution)/shard_map/ppermute | solution.py:536
  286.7 10.4 %collective-permute-done.3 = bf16[256,1536]{1,0:T(8,128)(2,1)} collective-permute-done((bf16[256,1536]{1,0:T(8,128)(2,1)}, bf16[256,1536]{1,0:T(8,128)(2,1)}, u32[]{:S(2)}, u32[]{:S(2)}) %collective-permute-start.3) | collective-permute-done | bytes 786464 | tf_op jit(solution)/shard_map/ppermute | solution.py:536
  297.1 18.3 %collective-permute-done.2 = bf16[256,1536]{1,0:T(8,128)(2,1)} collective-permute-done((bf16[256,1536]{1,0:T(8,128)(2,1)}, bf16[256,1536]{1,0:T(8,128)(2,1)}, u32[]{:S(2)}, u32[]{:S(2)}) %collective-permute-start.2) | collective-permute-done | bytes 786464 | tf_op jit(solution)/shard_map/ppermute | solution.py:536
  351.3 8.3 %convolution_convert_fusion.4 = bf16[1536,768]{1,0:T(8,128)(2,1)} fusion(bf16[2048,1536]{1,0:T(8,128)(2,1)S(1)} %bitcast.413, bf16[2048,768]{1,0:T(8,128)(2,1)} %get-tuple-element.51), kind=kOutput, calls=%fused_computation.22 | convolution fusion | flops 4833017856 | bytes 11796480 | tf_op jit(solution)/shard_map/dot_general | solution.py:29
  364.8 13.4 %collective-permute-start.22 = (bf16[2,192,768]{2,1,0:T(8,128)(2,1)}, bf16[2,192,768]{2,1,0:T(8,128)(2,1)S(1)}, u32[]{:S(2)}, u32[]{:S(2)}) collective-permute-start(bf16[2,192,768]{2,1,0:T(8,128)(2,1)} %get-tuple-element.84), channel_id=1, source_target_pairs={{2,0},{4,2},{6,4},{3,1},{5,3},{7,5},{10,8},{12,10},{14,12},{11,9},... | collective-permute-start | bytes 1769480 | tf_op jit(solution)/shard_map/ppermute | solution.py:578
  378.2 8.4 %convolution_convert_fusion.3 = bf16[1536,768]{1,0:T(8,128)(2,1)S(1)} fusion(bf16[2048,1536]{1,0:T(8,128)(2,1)} %bitcast.409, bf16[2048,768]{1,0:T(8,128)(2,1)} %copy-done.32), kind=kOutput, calls=%fused_computation.21 | convolution fusion | flops 4833017856 | bytes 11796480 | tf_op jit(solution)/shard_map/dot_general | solution.py:29
  391.9 8.1 %convolution_convert_fusion.2 = bf16[768,1536]{1,0:T(8,128)(2,1)S(1)} fusion(bf16[2048,768]{1,0:T(8,128)(2,1)S(1)} %copy-done.34, bf16[2048,1536]{1,0:T(8,128)(2,1)} %copy-done.14), kind=kOutput, calls=%fused_computation.20 | convolution fusion | flops 4833017856 | bytes 11796480 | tf_op jit(solution)/shard_map/dot_general | solution.py:29
  424.2 7.4 %collective-permute-done.20 = bf16[2,192,768]{2,1,0:T(8,128)(2,1)} collective-permute-done((bf16[2,192,768]{2,1,0:T(8,128)(2,1)S(1)}, bf16[2,192,768]{2,1,0:T(8,128)(2,1)}, u32[]{:S(2)}, u32[]{:S(2)}) %collective-permute-start.20) | collective-permute-done | bytes 589856 | tf_op jit(solution)/shard_map/ppermute | solution.py:577
  503.2 10.7 %collective-permute-done.42 = bf16[2,96,1536]{2,1,0:T(8,128)(2,1)S(1)} collective-permute-done((bf16[2,96,1536]{2,1,0:T(8,128)(2,1)S(1)}, bf16[2,96,1536]{2,1,0:T(8,128)(2,1)S(1)}, u32[]{:S(2)}, u32[]{:S(2)}) %collective-permute-start.42) | collective-permute-done | bytes 589856 | tf_op jit(solution)/shard_map/ppermute | solution.py:578
  515.8 25.8 %collective-permute-done.25 = bf16[192,768]{1,0:T(8,128)(2,1)S(1)} collective-permute-done((bf16[192,768]{1,0:T(8,128)(2,1)S(1)}, bf16[192,768]{1,0:T(8,128)(2,1)S(1)}, u32[]{:S(2)}, u32[]{:S(2)}) %collective-permute-start.25) | collective-permute-done | bytes 294944 | tf_op jit(solution)/shard_map/ppermute | solution.py:536
  555.6 10.0 %collective-permute-start.27 = (bf16[2,2,1,192,768]{4,3,0,1,2:T(8,128)(2,1)S(1)}, bf16[2,2,1,192,768]{4,3,0,1,2:T(8,128)(2,1)S(1)}, u32[]{:S(2)}, u32[]{:S(2)}) collective-permute-start(bf16[2,2,1,192,768]{4,3,0,1,2:T(8,128)(2,1)S(1)} %pad_maximum_fusion.2), channel_id=1, source_target_pairs={{0,8},{8,0},{1,9},{9,1},{2,10},{10,2},{3,11},{11,3},{4,12},{12,4},... | collective-permute-start | bytes 3538952 | tf_op jit(solution)/shard_map/ppermute | solution.py:536
  565.9 12.4 %collective-permute-start.36 = (bf16[2,2,1,192,768]{4,3,0,1,2:T(8,128)(2,1)S(1)}, bf16[2,2,1,192,768]{4,3,0,1,2:T(8,128)(2,1)S(1)}, u32[]{:S(2)}, u32[]{:S(2)}) collective-permute-start(bf16[2,2,1,192,768]{4,3,0,1,2:T(8,128)(2,1)S(1)} %pad_maximum_fusion.3), channel_id=1, source_target_pairs={{0,8},{8,0},{1,9},{9,1},{2,10},{10,2},{3,11},{11,3},{4,12},{12,4},... | collective-permute-start | bytes 3538952 | tf_op jit(solution)/shard_map/ppermute | solution.py:536
  578.3 14.3 %collective-permute-done.10 = bf16[4,48,3712]{2,1,0:T(8,128)(2,1)S(1)} collective-permute-done((bf16[4,48,3712]{2,1,0:T(8,128)(2,1)S(1)}, bf16[4,48,3712]{2,1,0:T(8,128)(2,1)S(1)}, u32[]{:S(2)}, u32[]{:S(2)}) %collective-permute-start.10) | collective-permute-done | bytes 1425440 | tf_op jit(solution)/shard_map/ppermute | solution.py:536
  595.6 9.6 %collective-permute-done.44 = bf16[2,1,96,1536]{3,2,0,1:T(8,128)(2,1)S(1)} collective-permute-done((bf16[2,1,96,1536]{3,2,0,1:T(8,128)(2,1)S(1)}, bf16[2,1,96,1536]{3,2,0,1:T(8,128)(2,1)S(1)}, u32[]{:S(2)}, u32[]{:S(2)}) %collective-permute-start.44) | collective-permute-done | bytes 589856 | tf_op jit(solution)/shard_map/ppermute | solution.py:536
  611.0 13.2 %collective-permute-start.45 = (bf16[2,2,1,96,1536]{4,3,0,1,2:T(8,128)(2,1)S(1)}, bf16[2,2,1,96,1536]{4,3,0,1,2:T(8,128)(2,1)S(1)}, u32[]{:S(2)}, u32[]{:S(2)}) collective-permute-start(bf16[2,2,1,96,1536]{4,3,0,1,2:T(8,128)(2,1)S(1)} %pad_maximum_fusion.4), channel_id=1, source_target_pairs={{0,8},{8,0},{1,9},{9,1},{2,10},{10,2},{3,11},{11,3},{4,12},{12,4},... | collective-permute-start | bytes 3538952 | tf_op jit(solution)/shard_map/ppermute | solution.py:536
  642.4 8.2 %collective-permute-start.17 = (bf16[48,3712]{1,0:T(8,128)(2,1)S(1)}, bf16[48,3712]{1,0:T(8,128)(2,1)S(1)}, u32[]{:S(2)}, u32[]{:S(2)}) collective-permute-start(bf16[48,3712]{1,0:T(8,128)(2,1)S(1)} %fusion.65), channel_id=1, source_target_pairs={{0,8},{8,0},{1,9},{9,1},{2,10},{10,2},{3,11},{11,3},{4,12},{12,4},... | collective-permute-start | bytes 1069064 | tf_op jit(solution)/shard_map/ppermute | solution.py:536
  660.7 8.7 %collective-permute-done.18 = bf16[2,48,3712]{2,1,0:T(8,128)(2,1)S(1)} collective-permute-done((bf16[2,48,3712]{2,1,0:T(8,128)(2,1)S(1)}, bf16[2,48,3712]{2,1,0:T(8,128)(2,1)S(1)}, u32[]{:S(2)}, u32[]{:S(2)}) %collective-permute-start.18) | collective-permute-done | bytes 712736 | tf_op jit(solution)/shard_map/ppermute | solution.py:536
  (278 shorter events, 246.7 us)
Async XLA Ops:
  245.7 37.5 %collective-permute-start.6 = (bf16[256,1536]{1,0:T(8,128)(2,1)}, bf16[256,1536]{1,0:T(8,128)(2,1)}, u32[]{:S(2)}, u32[]{:S(2)}) collective-permute-start(bf16[256,1536]{1,0:T(8,128)(2,1)} %get-tuple-element.59), channel_id=1, source_target_pairs={{0,16},{16,0},{1,17},{17,1},{2,18},{18,2},{3,19},{19,3},{4,20},{20... | collective-permute-start | bytes 2359304 | tf_op jit(solution)/shard_map/ppermute | solution.py:536
  245.9 37.2 %collective-permute-start.5 = (bf16[256,1536]{1,0:T(8,128)(2,1)}, bf16[256,1536]{1,0:T(8,128)(2,1)}, u32[]{:S(2)}, u32[]{:S(2)}) collective-permute-start(bf16[256,1536]{1,0:T(8,128)(2,1)} %get-tuple-element.57), channel_id=1, source_target_pairs={{0,1},{1,0},{2,3},{3,2},{4,5},{5,4},{6,7},{7,6},{8,9},{9,8},{10,11... | collective-permute-start | bytes 2359304 | tf_op jit(solution)/shard_map/ppermute | solution.py:536
  252.3 44.8 %collective-permute-start.3 = (bf16[256,1536]{1,0:T(8,128)(2,1)}, bf16[256,1536]{1,0:T(8,128)(2,1)}, u32[]{:S(2)}, u32[]{:S(2)}) collective-permute-start(bf16[256,1536]{1,0:T(8,128)(2,1)} %get-tuple-element.61), channel_id=1, source_target_pairs={{0,17},{1,16},{16,1},{17,0},{2,19},{3,18},{18,3},{19,2},{4,21},{5,... | collective-permute-start | bytes 2359304 | tf_op jit(solution)/shard_map/ppermute | solution.py:536
  253.6 61.8 %collective-permute-start.2 = (bf16[256,1536]{1,0:T(8,128)(2,1)}, bf16[256,1536]{1,0:T(8,128)(2,1)}, u32[]{:S(2)}, u32[]{:S(2)}) collective-permute-start(bf16[256,1536]{1,0:T(8,128)(2,1)} %get-tuple-element.62), channel_id=1, source_target_pairs={{0,16},{16,0},{1,17},{17,1},{2,18},{18,2},{3,19},{19,3},{4,20},{20... | collective-permute-start | bytes 2359304 | tf_op jit(solution)/shard_map/ppermute | solution.py:536
  263.2 52.2 %collective-permute-start.1 = (bf16[256,1536]{1,0:T(8,128)(2,1)}, bf16[256,1536]{1,0:T(8,128)(2,1)}, u32[]{:S(2)}, u32[]{:S(2)}) collective-permute-start(bf16[256,1536]{1,0:T(8,128)(2,1)} %get-tuple-element.60), channel_id=1, source_target_pairs={{0,1},{1,0},{2,3},{3,2},{4,5},{5,4},{6,7},{7,6},{8,9},{9,8},{10,11... | collective-permute-start | bytes 2359304 | tf_op jit(solution)/shard_map/ppermute | solution.py:536
  350.8 116.0 %collective-permute-start.8 = (bf16[2,2,4,48,3712]{4,3,1,0,2:T(8,128)(2,1)}, bf16[2,2,4,48,3712]{4,3,1,0,2:T(8,128)(2,1)}, u32[]{:S(2)}, u32[]{:S(2)}) collective-permute-start(bf16[2,2,4,48,3712]{4,3,1,0,2:T(8,128)(2,1)} %dynamic-slice_bitcast_fusion), channel_id=1, source_target_pairs={{0,8},{8,0},{1,9},{9,1},{2,10},{10,2},{3,11},{11,3},{4,12},{12,4},... | collective-permute-start | bytes 17104904 | tf_op jit(solution)/shard_map/ppermute | solution.py:536
  361.9 43.9 %collective-permute-start.19 = (bf16[2,192,768]{2,1,0:T(8,128)(2,1)}, bf16[2,192,768]{2,1,0:T(8,128)(2,1)}, u32[]{:S(2)}, u32[]{:S(2)}) collective-permute-start(bf16[2,192,768]{2,1,0:T(8,128)(2,1)} %get-tuple-element.83), channel_id=1, source_target_pairs={{0,2},{2,4},{4,6},{1,3},{3,5},{5,7},{8,10},{10,12},{12,14},{9,11},... | collective-permute-start | bytes 1769480 | tf_op jit(solution)/shard_map/ppermute | solution.py:577
  364.8 49.9 %collective-permute-start.22 = (bf16[2,192,768]{2,1,0:T(8,128)(2,1)}, bf16[2,192,768]{2,1,0:T(8,128)(2,1)S(1)}, u32[]{:S(2)}, u32[]{:S(2)}) collective-permute-start(bf16[2,192,768]{2,1,0:T(8,128)(2,1)} %get-tuple-element.84), channel_id=1, source_target_pairs={{2,0},{4,2},{6,4},{3,1},{5,3},{7,5},{10,8},{12,10},{14,12},{11,9},... | collective-permute-start | bytes 1769480 | tf_op jit(solution)/shard_map/ppermute | solution.py:578
  405.8 30.7 %collective-permute-start.31 = (bf16[2,192,768]{2,1,0:T(8,128)(2,1)}, bf16[2,192,768]{2,1,0:T(8,128)(2,1)}, u32[]{:S(2)}, u32[]{:S(2)}) collective-permute-start(bf16[2,192,768]{2,1,0:T(8,128)(2,1)} %get-tuple-element.78), channel_id=1, source_target_pairs={{2,0},{4,2},{6,4},{3,1},{5,3},{7,5},{10,8},{12,10},{14,12},{11,9},... | collective-permute-start | bytes 1769480 | tf_op jit(solution)/shard_map/ppermute | solution.py:578
  414.7 34.9 %collective-permute-start.40 = (bf16[2,96,1536]{2,1,0:T(8,128)(2,1)S(1)}, bf16[2,96,1536]{2,1,0:T(8,128)(2,1)}, u32[]{:S(2)}, u32[]{:S(2)}) collective-permute-start(bf16[2,96,1536]{2,1,0:T(8,128)(2,1)S(1)} %get-tuple-element.72), channel_id=1, source_target_pairs={{2,0},{4,2},{6,4},{3,1},{5,3},{7,5},{10,8},{12,10},{14,12},{11,9},... | collective-permute-start | bytes 1769480 | tf_op jit(solution)/shard_map/ppermute | solution.py:578
  418.9 25.3 %collective-permute-start.29 = (bf16[2,192,768]{2,1,0:T(8,128)(2,1)}, bf16[2,192,768]{2,1,0:T(8,128)(2,1)}, u32[]{:S(2)}, u32[]{:S(2)}) collective-permute-start(bf16[2,192,768]{2,1,0:T(8,128)(2,1)} %fusion.38), channel_id=1, source_target_pairs={{0,2},{2,4},{4,6},{1,3},{3,5},{5,7},{8,10},{10,12},{12,14},{9,11},... | collective-permute-start | bytes 1769480 | tf_op jit(solution)/shard_map/ppermute | solution.py:577
  431.5 25.3 %collective-permute-start.38 = (bf16[2,96,1536]{2,1,0:T(8,128)(2,1)}, bf16[2,96,1536]{2,1,0:T(8,128)(2,1)}, u32[]{:S(2)}, u32[]{:S(2)}) collective-permute-start(bf16[2,96,1536]{2,1,0:T(8,128)(2,1)} %fusion.32), channel_id=1, source_target_pairs={{0,2},{2,4},{4,6},{1,3},{3,5},{5,7},{8,10},{10,12},{12,14},{9,11},... | collective-permute-start | bytes 1769480 | tf_op jit(solution)/shard_map/ppermute | solution.py:577
  436.5 25.9 %collective-permute-start.23 = (bf16[2,192,768]{2,1,0:T(8,128)(2,1)S(1)}, bf16[2,192,768]{2,1,0:T(8,128)(2,1)S(1)}, u32[]{:S(2)}, u32[]{:S(2)}) collective-permute-start(bf16[2,192,768]{2,1,0:T(8,128)(2,1)S(1)} %get-tuple-element.82), channel_id=1, source_target_pairs={{2,0},{4,2},{6,4},{3,1},{5,3},{7,5},{10,8},{12,10},{14,12},{11,9},... | collective-permute-start | bytes 1769480 | tf_op jit(solution)/shard_map/ppermute | solution.py:578
  444.2 36.7 %collective-permute-start.21 = (bf16[2,192,768]{2,1,0:T(8,128)(2,1)S(1)}, bf16[2,192,768]{2,1,0:T(8,128)(2,1)S(1)}, u32[]{:S(2)}, u32[]{:S(2)}) collective-permute-start(bf16[2,192,768]{2,1,0:T(8,128)(2,1)S(1)} %get-tuple-element.81), channel_id=1, source_target_pairs={{0,2},{2,4},{4,6},{1,3},{3,5},{5,7},{8,10},{10,12},{12,14},{9,11},... | collective-permute-start | bytes 1769480 | tf_op jit(solution)/shard_map/ppermute | solution.py:577
  456.8 36.0 %collective-permute-start.30 = (bf16[2,192,768]{2,1,0:T(8,128)(2,1)S(1)}, bf16[2,192,768]{2,1,0:T(8,128)(2,1)S(1)}, u32[]{:S(2)}, u32[]{:S(2)}) collective-permute-start(bf16[2,192,768]{2,1,0:T(8,128)(2,1)S(1)} %get-tuple-element.75), channel_id=1, source_target_pairs={{0,2},{2,4},{4,6},{1,3},{3,5},{5,7},{8,10},{10,12},{12,14},{9,11},... | collective-permute-start | bytes 1769480 | tf_op jit(solution)/shard_map/ppermute | solution.py:577
  474.8 74.3 %collective-permute-start.9 = (bf16[2,4,48,3712]{3,2,0,1:T(8,128)(2,1)S(1)}, bf16[2,4,48,3712]{3,2,0,1:T(8,128)(2,1)S(1)}, u32[]{:S(2)}, u32[]{:S(2)}) collective-permute-start(bf16[2,4,48,3712]{3,2,0,1:T(8,128)(2,1)S(1)} %dynamic-slice_bitcast_fusion.1), channel_id=1, source_target_pairs={{0,1},{1,0},{2,3},{3,2},{4,5},{5,4},{6,7},{7,6},{8,9},{9,8},{10,11... | collective-permute-start | bytes 8552456 | tf_op jit(solution)/shard_map/ppermute | solution.py:536
  488.6 25.3 %collective-permute-start.42 = (bf16[2,96,1536]{2,1,0:T(8,128)(2,1)S(1)}, bf16[2,96,1536]{2,1,0:T(8,128)(2,1)S(1)}, u32[]{:S(2)}, u32[]{:S(2)}) collective-permute-start(bf16[2,96,1536]{2,1,0:T(8,128)(2,1)S(1)} %fusion.31), channel_id=1, source_target_pairs={{2,0},{4,2},{6,4},{3,1},{5,3},{7,5},{10,8},{12,10},{14,12},{11,9},... | collective-permute-start | bytes 1769480 | tf_op jit(solution)/shard_map/ppermute | solution.py:578
  492.8 48.8 %collective-permute-start.25 = (bf16[192,768]{1,0:T(8,128)(2,1)S(1)}, bf16[192,768]{1,0:T(8,128)(2,1)S(1)}, u32[]{:S(2)}, u32[]{:S(2)}) collective-permute-start(bf16[192,768]{1,0:T(8,128)(2,1)S(1)} %dynamic-slice_bitcast_fusion.13), channel_id=1, source_target_pairs={{0,1},{1,0},{2,3},{3,2},{4,5},{5,4},{6,7},{7,6},{8,9},{9,8},{10,11... | collective-permute-start | bytes 884744 | tf_op jit(solution)/shard_map/ppermute | solution.py:536
  501.5 46.5 %collective-permute-start.34 = (bf16[192,768]{1,0:T(8,128)(2,1)S(1)}, bf16[192,768]{1,0:T(8,128)(2,1)S(1)}, u32[]{:S(2)}, u32[]{:S(2)}) collective-permute-start(bf16[192,768]{1,0:T(8,128)(2,1)S(1)} %dynamic-slice_bitcast_fusion.12), channel_id=1, source_target_pairs={{0,1},{1,0},{2,3},{3,2},{4,5},{5,4},{6,7},{7,6},{8,9},{9,8},{10,11... | collective-permute-start | bytes 884744 | tf_op jit(solution)/shard_map/ppermute | solution.py:536
  514.1 40.2 %collective-permute-start.43 = (bf16[96,1536]{1,0:T(8,128)(2,1)S(1)}, bf16[96,1536]{1,0:T(8,128)(2,1)S(1)}, u32[]{:S(2)}, u32[]{:S(2)}) collective-permute-start(bf16[96,1536]{1,0:T(8,128)(2,1)S(1)} %dynamic-slice_bitcast_fusion.11), channel_id=1, source_target_pairs={{0,1},{1,0},{2,3},{3,2},{4,5},{5,4},{6,7},{7,6},{8,9},{9,8},{10,11... | collective-permute-start | bytes 884744 | tf_op jit(solution)/shard_map/ppermute | solution.py:536
  549.9 42.6 %collective-permute-start.10 = (bf16[4,48,3712]{2,1,0:T(8,128)(2,1)S(1)}, bf16[4,48,3712]{2,1,0:T(8,128)(2,1)S(1)}, u32[]{:S(2)}, u32[]{:S(2)}) collective-permute-start(bf16[4,48,3712]{2,1,0:T(8,128)(2,1)S(1)} %dynamic-slice_bitcast_fusion.2), channel_id=1, source_target_pairs={{0,16},{16,0},{1,17},{17,1},{2,18},{18,2},{3,19},{19,3},{4,20},{20... | collective-permute-start | bytes 4276232 | tf_op jit(solution)/shard_map/ppermute | solution.py:536
  554.4 50.8 %collective-permute-start.44 = (bf16[2,1,96,1536]{3,2,0,1:T(8,128)(2,1)S(1)}, bf16[2,1,96,1536]{3,2,0,1:T(8,128)(2,1)S(1)}, u32[]{:S(2)}, u32[]{:S(2)}) collective-permute-start(bf16[2,1,96,1536]{3,2,0,1:T(8,128)(2,1)S(1)} %maximum_bitcast_fusion.2), channel_id=1, source_target_pairs={{0,16},{16,0},{1,17},{17,1},{2,18},{18,2},{3,19},{19,3},{4,20},{20... | collective-permute-start | bytes 1769480 | tf_op jit(solution)/shard_map/ppermute | solution.py:536
  555.6 95.0 %collective-permute-start.27 = (bf16[2,2,1,192,768]{4,3,0,1,2:T(8,128)(2,1)S(1)}, bf16[2,2,1,192,768]{4,3,0,1,2:T(8,128)(2,1)S(1)}, u32[]{:S(2)}, u32[]{:S(2)}) collective-permute-start(bf16[2,2,1,192,768]{4,3,0,1,2:T(8,128)(2,1)S(1)} %pad_maximum_fusion.2), channel_id=1, source_target_pairs={{0,8},{8,0},{1,9},{9,1},{2,10},{10,2},{3,11},{11,3},{4,12},{12,4},... | collective-permute-start | bytes 3538952 | tf_op jit(solution)/shard_map/ppermute | solution.py:536
  565.9 84.9 %collective-permute-start.36 = (bf16[2,2,1,192,768]{4,3,0,1,2:T(8,128)(2,1)S(1)}, bf16[2,2,1,192,768]{4,3,0,1,2:T(8,128)(2,1)S(1)}, u32[]{:S(2)}, u32[]{:S(2)}) collective-permute-start(bf16[2,2,1,192,768]{4,3,0,1,2:T(8,128)(2,1)S(1)} %pad_maximum_fusion.3), channel_id=1, source_target_pairs={{0,8},{8,0},{1,9},{9,1},{2,10},{10,2},{3,11},{11,3},{4,12},{12,4},... | collective-permute-start | bytes 3538952 | tf_op jit(solution)/shard_map/ppermute | solution.py:536
  (65 other events, 830.3 us)

commit v3 on v2

--- a/solution.py
+++ b/solution.py
@@ -22,7 +22,7 @@
 F32 = jnp.float32
 BF16 = jnp.bfloat16
 MESH = pl.DeviceIdType.MESH
-VMEM_LIMIT = 60 * 2**20
+VMEM_LIMIT = 62 * 2**20
 
 
 def dot(a, b, dims):
@@ -65,8 +65,8 @@
     def slot(self, key):
         return self.slots.setdefault(key, len(self.slots))
 
-    def send(self, key, src, dst, device, cond=None):
-        recv, index = self.slot(key), self.count
+    def send(self, key, src, dst, device, cond=None, slot=None):
+        recv, index = self.slot(slot or key), self.count
         self.count += 1
 
         def build():
@@ -496,109 +496,664 @@
     )(*args)
 
 
-def norm_back(values, scale_gain, upstream):
-    inverse = lax.rsqrt(jnp.mean(values * values, axis=-1, keepdims=True) + epsilon)
+class SlabReturn:
+    def __init__(self, net, name, coords, parts, length, mates, chips, load):
+        self.net, self.name, self.parts, self.length = net, name, parts, length
+        self.mates, self.landed, self.load = mates, chips, load
+        x, y, c, _ = coords
+        self.away = {1: {"y": 1 - y}, 2: {"x": 1 - x}, 3: {"y": 1 - y, "x": 1 - x}}
+        self.mate = {"c": 1 - c}
+
+    def part(self, slot):
+        return self.parts.at[slot * self.length : (slot + 1) * self.length, :]
+
+    def to_mate(self, chip):
+        self.net.send(
+            (self.name, "mate", chip),
+            lambda: self.part(2 * chip + 1),
+            lambda: self.mates.at[chip],
+            self.mate,
+        )
+
+    def fetch_mate(self, chip):
+        self.net.arrive((self.name, "mate", chip), lambda: self.mates.at[chip])
+        self.net.local((self.name, "load", chip), self.mates.at[chip], self.load.at[chip])
+
+    def to_chip(self, chip):
+        self.net.ready((self.name, "load", chip))
+        part = self.part(2 * chip)
+        accumulate(part, part, self.load.at[chip])
+        self.net.send(
+            (self.name, "chip", chip),
+            lambda: part,
+            lambda: self.landed.at[chip - 1],
+            self.away[chip],
+        )
+
+    def total(self, out, *more):
+        self.fetch_mate(0)
+        for chip in (1, 2, 3):
+            self.net.arrive((self.name, "chip", chip), lambda: self.landed.at[chip - 1])
+            self.net.local((self.name, "last", chip), self.landed.at[chip - 1], self.load.at[chip])
+        self.net.ready((self.name, "load", 0))
+        for chip in (1, 2, 3):
+            self.net.ready((self.name, "last", chip))
+        accumulate(out, self.part(0), *(self.load.at[chip] for chip in range(4)), *more)
+
+    def sent(self):
+        for chip in range(4):
+            self.net.sent((self.name, "mate", chip))
+            if chip:
+                self.net.sent((self.name, "chip", chip))
+
+
+def accumulate(out, *terms):
+    total, columns = out.shape
+    step = 32 if columns < 1024 and total % 32 == 0 else 16
+
+    @pl.loop(0, total // step)
+    def _(i):
+        here = pl.ds(pl.multiple_of(i * step, step), step)
+        value = terms[0][here, :].astype(F32)
+        for term in terms[1:]:
+            value = value + term[here, :].astype(F32)
+        out[here, :] = value.astype(out.dtype)
+
+
+def clear(out):
+    @pl.loop(0, out.shape[0] // 16)
+    def _(i):
+        here = pl.ds(pl.multiple_of(i * 16, 16), 16)
+        out[here, :] = jnp.zeros((16, out.shape[1]), out.dtype)
+
+
+class LineScatter:
+    def __init__(self, net, name, depth, z, block, landed, load):
+        self.net, self.name, self.depth, self.z = net, name, depth, z
+        self.block, self.landed, self.load = block, landed, load
+
+        steps = range(1, depth)
+        up = {s: (depth - s + z, z == 0, jnp.logical_and(z >= 1, z <= s - 1)) for s in steps}
+        back = depth - 1 - z
+        down = {s: (z + s - depth, back == 0, jnp.logical_and(back >= 1, back <= s - 1)) for s in steps}
+        self.ways = (
+            ("up", {"z": z + 1}, 0, z >= 1, z < 1, up),
+            ("down", {"z": z - 1}, 1, back >= 1, back < 1, down),
+        )
+
+    def send(self, key, device, way, s, t, cond):
+        self.net.send(
+            key,
+            lambda: self.block(t),
+            lambda: self.landed.at[way, s - 1],
+            device,
+            cond,
+            slot=(self.name, key[1], s),
+        )
+
+    def start(self):
+        for s in range(1, self.depth):
+            for tag, device, way, _, _, steps in self.ways:
+                target, first, _ = steps[s]
+                self.send((self.name, tag, s), device, way, s, target, first)
+
+    def term(self, way, s):
+        return self.landed.at[way, s - 1] if self.load is None else self.load.at[way]
+
+    def take(self, tag, way, s):
+        self.net.arrive((self.name, tag, s), lambda: self.landed.at[way, s - 1])
+        if self.load is not None:
+            pltpu.sync_copy(self.landed.at[way, s - 1], self.load.at[way])
+
+    def step(self, s):
+        for tag, device, way, _, _, steps in self.ways:
+            t, _, cond = steps[s]
+
+            def body():
+                self.take(tag, way, s - 1)
+                block = self.block(t)
+                accumulate(block, block, self.term(way, s - 1))
+
+            pl.when(cond)(body)
+            self.send((self.name, tag, s, "on"), device, way, s, t, cond)
+
+    def finish(self, *outs):
+        last = self.depth - 1
+        for tag, _, way, fed, unfed, _ in self.ways:
+            pl.when(fed)(lambda: self.take(tag, way, last))
+            pl.when(unfed)(lambda: clear(self.term(way, last)))
+        rows = outs[0].shape[0]
+        for i, out in enumerate(outs):
+            here = pl.ds(i * rows, rows)
+            accumulate(
+                out, *(term.at[here, :] for term in (self.block(self.z), self.term(0, last), self.term(1, last)))
+            )
+
+
+class ExpertShare:
+    def __init__(self, net, name, coords, result, dst):
+        self.net, self.name, self.coords, self.result, self.dst = net, name, coords, result, dst
+        x, y, c, _ = coords
+        self.expert = 4 * x + 2 * y + c
+        self.across = {4: {"x": 1 - x}, 2: {"y": 1 - y}, 1: {"c": 1 - c}}
+
+    def place(self, flip):
+        x, y, c, _ = self.coords
+        fx = 1 - x if flip & 4 else x
+        fy = 1 - y if flip & 2 else y
+        fc = 1 - c if flip & 1 else c
+        return self.dst.at[4 * fx + 2 * fy + fc]
+
+    def put(self, flip, src, axis):
+        self.net.send(
+            (self.name, axis | flip), src, lambda: self.place(flip), self.across[axis]
+        )
+
+    def wait(self, flip):
+        self.net.arrive((self.name, flip), lambda: self.place(flip))
+
+    def start(self):
+        x = self.coords[0]
+        own = lambda: self.result.at[x]
+        self.put(0, lambda: self.result.at[1 - x], 4)
+        self.put(0, own, 2)
+        self.put(0, own, 1)
+        self.net.local((self.name, "own"), own(), self.place(0))
+
+    def pass_x(self):
+        self.wait(4)
+        self.put(4, lambda: self.place(4), 2)
+        self.put(4, lambda: self.place(4), 1)
+
+    def pass_y(self):
+        for flip in (2, 6):
+            self.wait(flip)
+            self.put(flip, lambda: self.place(flip), 1)
+
+    def finish(self):
+        self.net.ready((self.name, "own"))
+        for flip in (1, 5, 3, 7):
+            self.wait(flip)
+
+
+class AttentionScatter:
+    def __init__(self, net, name, depth, coords, grad, mates, chips, lines, dst, mate_load, chip_load, blocks, low):
+        self.net, self.name, self.depth, self.coords = net, name, depth, coords
+        self.grad, self.mates, self.chips, self.dst = grad, mates, chips, dst
+        self.blocks, self.low = blocks, low
+        self.columns = columns = grad.shape[1] // 4
+        self.rows = grad.shape[0] // (2 * depth)
+        self.mate_load, self.chip_load = mate_load.at[:, :columns], chip_load.at[:, :, :, :columns]
+        x, y, c, z = coords
+        self.away = (
+            (1, x, 1 - y, {"y": 1 - y}),
+            (2, 1 - x, y, {"x": 1 - x}),
+            (3, 1 - x, 1 - y, {"y": 1 - y, "x": 1 - x}),
+        )
+        self.line = LineScatter(net, name + " line", depth, z, lambda t: blocks.at[t], lines, None)
+
+    def lanes(self, yi, ci):
+        return pl.ds(pl.multiple_of((2 * yi + ci) * self.columns, LANES), self.columns)
+
+    def part(self, zi, xi, yi):
+        rows = pl.ds(pl.multiple_of((zi * 2 + xi) * self.rows, self.rows), self.rows)
+        return self.grad.at[rows, self.lanes(yi, self.coords[2])]
+
+    def to_mate(self, j, yi):
+        c = self.coords[2]
+        self.net.send(
+            (self.name, "c", j),
+            lambda: self.grad.at[:, self.lanes(yi, 1 - c)],
+            lambda: self.mates.at[j],
+            {"c": 1 - c},
+        )
+
+    def to_chip(self, chip, zi, xi, yi, device):
+        self.net.send(
+            (self.name, chip, zi),
+            lambda: self.part(zi, xi, yi),
+            lambda: self.chips.at[chip - 1, zi],
+            device,
+        )
+
+    def start(self):
+        y = self.coords[1]
+        self.to_mate(1, 1 - y)
+        self.to_mate(0, y)
+
+    def pass_c(self):
+        x, y, c, z = self.coords
+        for j, yi in ((1, 1 - y), (0, y)):
+            self.net.arrive((self.name, "c", j), lambda: self.mates.at[j])
+            pltpu.sync_copy(self.mates.at[j], self.mate_load)
+            mine = self.grad.at[:, self.lanes(yi, c)]
+            accumulate(mine, mine, self.mate_load)
+            for chip, xi, yj, device in self.away:
+                if (chip in (1, 3)) == (j == 1):
+                    for zi in range(self.depth):
+                        self.to_chip(chip, zi, xi, yj, device)
+
+    def pass_chips(self):
+        x, y, c, z = self.coords
+        for chip, _, _, _ in self.away:
+            for zi in range(self.depth):
+                self.net.arrive((self.name, chip, zi), lambda: self.chips.at[chip - 1, zi])
+            self.net.local(
+                (self.name, "load", chip), self.chips.at[chip - 1], self.chip_load.at[chip - 1]
+            )
+        for chip, _, _, _ in self.away:
+            self.net.ready((self.name, "load", chip))
+        for zi in range(self.depth):
+            accumulate(
+                self.blocks.at[zi],
+                self.part(zi, x, y),
+                *(self.chip_load.at[chip, zi] for chip in range(3)),
+            )
+        self.line.start()
+
+    def total(self):
+        x, y, c, z = self.coords
+        self.line.finish(self.low)
+        mine = 2 * y + c
+        self.net.local((self.name, "own"), self.low, self.dst.at[mine])
+        for key, device in (("ty", {"y": 1 - y}), ("tc", {"c": 1 - c})):
+            self.net.send(
+                (self.name, key), lambda: self.low, lambda: self.dst.at[mine], device
+            )
+
+    def pass_y(self):
+        x, y, c, z = self.coords
+        there = 2 * (1 - y) + c
+        self.net.arrive((self.name, "ty"), lambda: self.dst.at[there])
+        self.net.send(
+            (self.name, "tyc"), lambda: self.dst.at[there], lambda: self.dst.at[there], {"c": 1 - c}
+        )
+
+    def finish(self):
+        x, y, c, z = self.coords
+        self.net.ready((self.name, "own"))
+        self.net.arrive((self.name, "tc"), lambda: self.dst.at[2 * y + 1 - c])
+        self.net.arrive((self.name, "tyc"), lambda: self.dst.at[2 * (1 - y) + 1 - c])
+
+
+def norm_back(values, gain, upstream):
+    inverse = inverse_rms(values)
     normal = values * inverse
-    gain_grad = jnp.sum(upstream * normal, axis=0)
-    scaled = upstream * scale_gain
-    value_grad = inverse * (scaled - normal * jnp.mean(scaled * normal, axis=-1, keepdims=True))
-    return (value_grad, gain_grad)
-
-
-def rms_norm(values, scale_gain):
+    gain_grad = jnp.sum(upstream * normal, axis=0, keepdims=True)
+    scaled = upstream * gain
     return (
-        values * lax.rsqrt(jnp.mean(values * values, axis=-1, keepdims=True) + epsilon) * scale_gain
+        inverse * (scaled - normal * jnp.mean(scaled * normal, axis=-1, keepdims=True)),
+        gain_grad,
     )
+
+
+def backward_kernel(depth, *refs):
+    (
+        hidden, grad_out, cosine, sine, gain_rows, queries, keys, values, attended, mixed,
+        probability, rows_in, grads_in, shares_in, gate_in, up_in, down_in, wq_in, wo_in,
+        layer_out, grad_in, gain_total,
+        gate_total, up_total, down_total, wq_total, wo_total,
+        row_mates, row_chips, out_mates, out_chips,
+        gate_lines, up_lines, down_lines, wq_mates, wq_chips, wo_mates, wo_chips,
+        rows, grads, wide, down_grad, returned, wide_load, down_load, wide_low, down_low,
+        mate_load, chip_load, wq_lines, wo_lines, wq_blocks, wo_blocks, wq_low, wo_low, gain_swap,
+        send_sems, recv_sems, local_sems,
+    ) = refs
+    coords = x, y, c, z = tuple(lax.axis_index(n) for n in ("x", "y", "c", "z"))
+    expert = 4 * x + 2 * y + c
+    net = Net(send_sems, recv_sems, local_sems, c)
+    length, width = hidden.shape
+    hidden_units = gate_in.shape[1]
+    greet(depth, coords)
+
+    def line(name, block, landed, load):
+        return LineScatter(net, name, depth, z, block, landed, load)
+
+    def wide_block(first):
+        size = 2 * (width // (2 * depth))
+        return lambda t: wide.at[
+            pl.ds(pl.multiple_of(t * size, size), size), pl.ds(first, hidden_units)
+        ]
+
+    def down_block(t):
+        size = 2 * (hidden_units // (2 * depth))
+        return down_grad.at[pl.ds(pl.multiple_of(t * size, size), size), :]
+
+    gate_line = line("gate", wide_block(0), gate_lines, wide_load)
+    up_line = line("up", wide_block(hidden_units), up_lines, wide_load)
+    down_line = line("down", down_block, down_lines, down_load)
+    row_back = SlabReturn(net, "rows", coords, grads, length, row_mates, row_chips, returned)
+    out_back = SlabReturn(net, "outs", coords, rows, length, out_mates, out_chips, returned)
+
+    def shared_out(name, line, low, dst):
+        def go():
+            line.finish(low.at[0], low.at[1])
+            share = ExpertShare(net, name + " share", coords, low, dst)
+            share.start()
+            return share
+
+        return go
+
+    down_done = shared_out("down", down_line, down_low, down_total)
+    gate_done = shared_out("gate", gate_line, wide_low.at[0], gate_total)
+    up_done = shared_out("up", up_line, wide_low.at[1], up_total)
+    tile = 256
+
+    def experts(down, hidden_act, both_grads, shares):
+        net.local("rows", rows_in, rows)
+        net.local("gate", gate_in, wide.at[:, :hidden_units])
+        net.local("up", up_in, wide.at[:, hidden_units:])
+        net.local("shares", shares_in, shares)
+        net.local("grads", grads_in, grads)
+        net.local("down", down_in, down)
+        for name in ("rows", "gate", "up", "shares", "grads", "down"):
+            net.ready(name)
+        lane = lax.broadcasted_iota(jnp.int32, (length, LANES), 1)
+
+        def share_of(r):
+            return jnp.sum(jnp.where(lane == expert, shares[r], 0.0), axis=1, keepdims=True)
+
+        @pl.loop(0, EXPERTS)
+        def _(r):
+            here = pl.ds(pl.multiple_of(r * length, length), length)
+            grads[here, :] = (share_of(r) * grads[here, :].astype(F32)).astype(BF16)
+            for j in range(0, hidden_units, tile):
+                gate = dot_nn(rows[here, :], wide[:, j : j + tile])
+                up = dot_nn(rows[here, :], wide[:, hidden_units + j : hidden_units + j + tile])
+                back = dot_nt(grads[here, :], down[j : j + tile, :])
+                sigmoid = 1.0 / (1.0 + jnp.exp(-gate))
+                silu = gate * sigmoid
+                hidden_act[here, j : j + tile] = (silu * up).astype(BF16)
+                both_grads[here, j : j + tile] = (
+                    back * up * sigmoid * (1.0 + gate * (1.0 - sigmoid))
+                ).astype(BF16)
+                both_grads[here, hidden_units + j : hidden_units + j + tile] = (
+                    back * silu
+                ).astype(BF16)
+
+        @pl.loop(0, hidden_units // tile)
+        def _(i):
+            at = pl.ds(pl.multiple_of(i * tile, tile), tile)
+            for j in range(0, width, 512):
+                down_grad[at, j : j + 512] = dot_tn(hidden_act[:, at], grads[:, j : j + 512]).astype(BF16)
+
+        down_line.start()
+
+        def row_grad(slot):
+            here = slice(slot * length, (slot + 1) * length)
+            for j in range(0, width, 512):
+                grads[here, j : j + 512] = dot_nt(both_grads[here, :], wide[j : j + 512, :]).astype(BF16)
+
+        for chip in (1, 2, 3, 0):
+            row_grad(2 * chip + 1)
+            row_back.to_mate(chip)
+        for chip in (1, 2, 3):
+            row_grad(2 * chip)
+            row_back.fetch_mate(chip)
+            row_back.to_chip(chip)
+        row_grad(0)
+
+        @pl.loop(0, width // tile)
+        def _(i):
+            at = pl.ds(pl.multiple_of(i * tile, tile), tile)
+            for j in range(0, 2 * hidden_units, 512):
+                wide[at, j : j + 512] = dot_tn(rows[:, at], both_grads[:, j : j + 512]).astype(BF16)
+
+        gate_line.start()
+        up_line.start()
+        for s in range(2, depth):
+            down_line.step(s)
+
+        def out_rows(slot):
+            here = slice(slot * length, (slot + 1) * length)
+            share = share_of(slot)
+            for j in range(0, width, 512):
+                rows[here, j : j + 512] = (
+                    share * dot_nn(hidden_act[here, :], down[:, j : j + 512])
+                ).astype(BF16)
+
+        for chip in (1, 2, 3, 0):
+            out_rows(2 * chip + 1)
+            out_back.to_mate(chip)
+        for chip in (1, 2, 3):
+            out_rows(2 * chip)
+            out_back.fetch_mate(chip)
+            out_back.to_chip(chip)
+        out_rows(0)
+
+    pl.run_scoped(
+        experts,
+        pltpu.VMEM((hidden_units, width), BF16),
+        pltpu.VMEM((EXPERTS * length, hidden_units), BF16),
+        pltpu.VMEM((EXPERTS * length, 2 * hidden_units), BF16),
+        pltpu.VMEM((EXPERTS, length, LANES), F32),
+    )
+
+    def attention(weight, chances, wq_grad, upstream_two, mixed_grad, mixed_low, attended_grad, qkv_grad):
+        net.local("wo here", wo_in, weight.at[:, :width])
+        net.local("chance 0", probability.at[: GROUP * length], chances)
+        row_back.total(upstream_two)
+        gain_swap[0] = jnp.zeros(gain_swap.shape[1:], F32)
+        step = 16
+
+        @pl.loop(0, length // step)
+        def _(i):
+            here = pl.ds(pl.multiple_of(i * step, step), step)
+            part, gain_two = norm_back(mixed[here, :], gain_rows[1:2, :], upstream_two[here, :])
+            total = grad_out[here, :].astype(F32) + part
+            mixed_grad[here, :] = total
+            mixed_low[here, :] = total.astype(BF16)
+            gain_swap[0, 1:2, :] += gain_two
+
+        row_back.sent()
+        for i in range(0, width, tile):
+            for j in range(0, width, 512):
+                grads[i : i + tile, j : j + 512] = dot_tn(
+                    attended[:, i : i + tile], mixed_low[:, j : j + 512]
+                ).astype(BF16)
+        wo_net = AttentionScatter(
+            net, "wo", depth, coords, grads.at[:width, :], wo_mates, wo_chips, wo_lines, wo_total,
+            mate_load, chip_load, wo_blocks, wo_low,
+        )
+        wo_net.start()
+        net.ready("wo here")
+        for i in range(0, width, 512):
+            attended_grad[:, i : i + 512] = dot_nt(
+                mixed_low[...], weight[i : i + 512, :width]
+            ).astype(BF16)
+        net.local("wq here", wq_in, weight)
+        down_share = down_done()
+        wo_net.pass_c()
+        for s in range(2, depth):
+            gate_line.step(s)
+        cos, sin = cosine[...], -sine[...]
+        factor = HEAD_DIM ** (-0.5)
+        for kv in range(KV_HEADS):
+            net.ready("chance %d" % kv)
+            there = slice(kv * length, (kv + 1) * length)
+            value_sum = key_sum = None
+            for g in range(GROUP):
+                head = kv * GROUP + g
+                here = slice(head * length, (head + 1) * length)
+                cols = slice(head * HEAD_DIM, (head + 1) * HEAD_DIM)
+                chance = chances[g * length : (g + 1) * length, :]
+                back = attended_grad[:, cols]
+                prob_grad = dot_nt(back, values[there, :])
+                value_part = dot_tn(chance.astype(BF16), back)
+                inner = jnp.sum(chance * prob_grad, axis=-1, keepdims=True)
+                score_grad = (chance * (prob_grad - inner)).astype(BF16)
+                query_grad = dot_nn(score_grad, keys[there, :]) * factor
+                key_part = dot_tn(score_grad, queries[here, :])
+                qkv_grad[:, cols] = turn(query_grad, cos, sin).astype(BF16)
+                value_sum = value_part if value_sum is None else value_sum + value_part
+                key_sum = key_part if key_sum is None else key_sum + key_part
+            if kv + 1 < KV_HEADS:
+                size = GROUP * length
+                net.local("chance %d" % (kv + 1), probability.at[(kv + 1) * size : (kv + 2) * size], chances)
+            first = (HEADS + kv) * HEAD_DIM
+            qkv_grad[:, first : first + HEAD_DIM] = turn(key_sum * factor, cos, sin).astype(BF16)
+            first = first + KV_HEADS * HEAD_DIM
+            qkv_grad[:, first : first + HEAD_DIM] = value_sum.astype(BF16)
+        down_share.pass_x()
+        @pl.loop(0, length // step)
+        def _(i):
+            here = pl.ds(pl.multiple_of(i * step, step), step)
+            one = hidden[here, :].astype(F32)
+            mixed_low[here, :] = (one * inverse_rms(one) * gain_rows[0:1, :]).astype(BF16)
+
+        for i in range(0, width, tile):
+            for j in range(0, wq_grad.shape[1], 512):
+                wq_grad[i : i + tile, j : j + 512] = dot_tn(
+                    mixed_low[:, i : i + tile], qkv_grad[:, j : j + 512]
+                ).astype(BF16)
+        wq_net = AttentionScatter(
+            net, "wq", depth, coords, wq_grad, wq_mates, wq_chips, wq_lines, wq_total,
+            mate_load, chip_load, wq_blocks, wq_low,
+        )
+        wq_net.start()
+        net.ready("wq here")
+        for i in range(0, width, 512):
+            upstream_two[:, i : i + 512] = dot_nt(qkv_grad[...], weight[i : i + 512, :])
+
+        @pl.loop(0, length // step)
+        def _(i):
+            here = pl.ds(pl.multiple_of(i * step, step), step)
+            part, gain_one = norm_back(
+                hidden[here, :].astype(F32), gain_rows[0:1, :], upstream_two[here, :]
+            )
+            grad_in[here, :] = (mixed_grad[here, :] + part).astype(BF16)
+            gain_swap[0, 0:1, :] += gain_one
+
+        wq_net.pass_c()
+        wo_net.pass_chips()
+        for i, (axis, device) in enumerate(
+            (("c", {"c": 1 - c}), ("x", {"x": 1 - x}), ("y", {"y": 1 - y}))
+        ):
+            source, target = gain_swap.at[2 * i], gain_swap.at[2 * i + 1]
+            gain_send(("gain", axis), source, target, device)
+            net.arrive(("gain", axis), lambda: target)
+            gain_swap[2 * i + 2] = gain_swap[2 * i] + gain_swap[2 * i + 1]
+        for far in range(1, depth):
+            gain_send(("gain", "up", far), gain_swap.at[6], gain_swap.at[5 + 2 * far], {"z": z + far}, z + far < depth)
+            gain_send(("gain", "down", far), gain_swap.at[6], gain_swap.at[6 + 2 * far], {"z": z - far}, z - far >= 0)
+        for s in range(2, depth):
+            up_line.step(s)
+        for s in range(2, depth):
+            wo_net.line.step(s)
+        out_back.total(layer_out, mixed)
+        wq_net.pass_chips()
+        gate_share = gate_done()
+        down_share.pass_y()
+        wo_net.total()
+        for s in range(2, depth):
+            wq_net.line.step(s)
+        up_share = up_done()
+        gate_share.pass_x()
+        wo_net.pass_y()
+        gain_total[...] = gain_swap[6]
+        for far in range(1, depth):
+            for tag, slot, cond in (
+                ("up", 5 + 2 * far, z - far >= 0), ("down", 6 + 2 * far, z + far < depth)
+            ):
+
+                def take():
+                    net.arrive(("gain", tag, far), lambda: gain_swap.at[slot])
+                    gain_total[...] += gain_swap[slot]
+
+                pl.when(cond)(take)
+        wq_net.total()
+        up_share.pass_x()
+        gate_share.pass_y()
+        wq_net.pass_y()
+        up_share.pass_y()
+        for one in (down_share, gate_share, up_share, wo_net, wq_net):
+            one.finish()
+        net.drain()
+
+    def gain_send(key, source, target, device, cond=None):
+        net.send(key, lambda: source, lambda: target, device, cond)
+
+    pl.run_scoped(
+        attention,
+        pltpu.VMEM(wq_in.shape, BF16),
+        pltpu.VMEM((GROUP * length, length), F32),
+        pltpu.VMEM(wq_in.shape, BF16),
+        pltpu.VMEM((length, width), F32),
+        pltpu.VMEM((length, width), F32),
+        pltpu.VMEM((length, width), BF16),
+        pltpu.VMEM((length, width), BF16),
+        pltpu.VMEM((length, wq_in.shape[1]), BF16),
+    )
+    assert net.count <= send_sems.shape[0] and len(net.slots) <= recv_sems.shape[0]
+    assert len(net.locals) <= local_sems.shape[0]
+
+
+def backward_call(depth, shard_rows, *args):
+    hidden, wq_in, gate_in, down_in = args[0], args[17], args[14], args[16]
+    length, width = hidden.shape
+    wide, units = wq_in.shape[1], gate_in.shape[1]
+    shards, down_rows = 2 * depth, units // (2 * depth)
+    here, there = pl.BlockSpec(memory_space=pltpu.VMEM), pl.BlockSpec(memory_space=pltpu.HBM)
+
+    def shape(*dims, dtype=BF16):
+        return jax.ShapeDtypeStruct(dims, dtype)
+
+    out_shape = [
+        shape(length, width), shape(length, width), shape(8, width, dtype=F32),
+        shape(EXPERTS, shard_rows, units), shape(EXPERTS, shard_rows, units),
+        shape(EXPERTS, down_rows, width),
+        shape(4, shard_rows, wide // 4), shape(4, shard_rows, width // 4),
+        shape(4, length, width), shape(3, length, width),
+        shape(4, length, width), shape(3, length, width),
+        shape(2, depth - 1, 2 * shard_rows, units), shape(2, depth - 1, 2 * shard_rows, units),
+        shape(2, depth - 1, 2 * down_rows, width),
+        shape(2, width, wide // 4), shape(3, depth, shard_rows, wide // 4),
+        shape(2, width, width // 4), shape(3, depth, shard_rows, width // 4),
+    ]
+    sends = 60 * depth + 160
+    return pl.pallas_call(
+        functools.partial(backward_kernel, depth),
+        out_shape=out_shape,
+        in_specs=[here] * 10 + [there] * 9,
+        out_specs=[here] * 3 + [there] * 16,
+        scratch_shapes=[
+            pltpu.VMEM((EXPERTS * length, width), BF16),
+            pltpu.VMEM((EXPERTS * length, width), BF16),
+            pltpu.VMEM((width, 2 * units), BF16),
+            pltpu.VMEM((units, width), BF16),
+            pltpu.VMEM((4, length, width), BF16),
+            pltpu.VMEM((2, 2 * shard_rows, units), BF16),
+            pltpu.VMEM((2, 2 * down_rows, width), BF16),
+            pltpu.VMEM((2, 2, shard_rows, units), BF16),
+            pltpu.VMEM((2, down_rows, width), BF16),
+            pltpu.VMEM((width, wide // 4), BF16),
+            pltpu.VMEM((3, depth, shard_rows, wide // 4), BF16),
+            pltpu.VMEM((2, depth - 1, shard_rows, wide // 4), BF16),
+            pltpu.VMEM((2, depth - 1, shard_rows, width // 4), BF16),
+            pltpu.VMEM((depth, shard_rows, wide // 4), BF16),
+            pltpu.VMEM((depth, shard_rows, width // 4), BF16),
+            pltpu.VMEM((shard_rows, wide // 4), BF16),
+            pltpu.VMEM((shard_rows, width // 4), BF16),
+            pltpu.VMEM((5 + 2 * depth, 8, width), F32),
+            pltpu.SemaphoreType.DMA((sends,)),
+            pltpu.SemaphoreType.DMA((sends,)),
+            pltpu.SemaphoreType.DMA((64,)),
+        ],
+        compiler_params=pltpu.CompilerParams(
+            collective_id=2, has_side_effects=True, vmem_limit_bytes=VMEM_LIMIT
+        ),
+    )(*args)
 
 
 def rotary_tables(length, head_width):
     half_width = head_width // 2
     frequency = rotary_base ** (-2.0 * jnp.arange(half_width, dtype=jnp.float32) / head_width)
     angles = jnp.arange(length, dtype=jnp.float32)[:, None] * frequency[None, :]
-    return (jnp.cos(angles)[:, None, :], jnp.sin(angles)[:, None, :])
-
-
-def rotate(values, cosine, sine_table):
-    half_width = values.shape[-1] // 2
-    first_half = values[..., :half_width]
-    second_half = values[..., half_width:]
-    return jnp.concatenate(
-        [
-            first_half * cosine - second_half * sine_table,
-            second_half * cosine + first_half * sine_table,
-        ],
-        axis=-1,
+    cosine, sine = jnp.cos(angles), jnp.sin(angles)
+    return (
+        jnp.concatenate([cosine, cosine], axis=1),
+        jnp.concatenate([-sine, sine], axis=1),
     )
-
-
-def swap(value, axes):
-    count = 2 ** len(axes)
-    return lax.ppermute(value, axes, [(i, count - 1 - i) for i in range(count)])
-
-
-def ordered(mine, other, place):
-    first = jnp.where(place == 0, mine, other)
-    second = jnp.where(place == 0, other, mine)
-    return jnp.stack([first, second])
-
-
-def line_steps(depth):
-    up = [(i, i + 1) for i in range(depth - 1)]
-    down = [(i + 1, i) for i in range(depth - 1)]
-    return up, down
-
-
-def line_gather(block, depth, place):
-    up, down = line_steps(depth)
-    below, above = [], []
-    a = b = block
-    for _ in range(depth - 1):
-        a = lax.ppermute(a, "z", up)
-        b = lax.ppermute(b, "z", down)
-        below.append(a)
-        above.append(b)
-    around = jnp.stack(below[::-1] + [block] + above)
-    return lax.dynamic_slice_in_dim(around, depth - 1 - place, depth, 0)
-
-
-def line_scatter(blocks, depth, place):
-    up, down = line_steps(depth)
-
-    def at(index):
-        return lax.dynamic_index_in_dim(blocks, jnp.clip(index, 0, depth - 1), 0, keepdims=False)
-
-    a = b = None
-    for step in range(1, depth):
-        send_a = at(depth - step + place)
-        send_b = at(place - 1 - (depth - 1) + step - 0)
-        if a is not None:
-            send_a = (send_a.astype(F32) + a.astype(F32)).astype(BF16)
-            send_b = (send_b.astype(F32) + b.astype(F32)).astype(BF16)
-        a = lax.ppermute(send_a, "z", up)
-        b = lax.ppermute(send_b, "z", down)
-    total = at(place).astype(F32)
-    if a is not None:
-        total = total + a.astype(F32) + b.astype(F32)
-    return total
-
-
-def slab_gather(block):
-    by_x = swap(block, ("x",))
-    by_y = swap(block, ("y",))
-    by_xy = swap(block, ("y", "x"))
-    chips = jnp.stack([block, by_y, by_x, by_xy])
-    mate = swap(chips, ("c",))
-    return jnp.stack([chips, mate], axis=1)
-
-
-def slab_return(parts):
-    mate = swap(parts[:, 1], ("c",))
-    both = parts[:, 0].astype(F32) + mate.astype(F32)
-    low = both.astype(BF16)
-    by_y = swap(low[1], ("y",))
-    by_x = swap(low[2], ("x",))
-    by_xy = swap(low[3], ("y", "x"))
-    return both[0] + by_x.astype(F32) + by_y.astype(F32) + by_xy.astype(F32)
 
 
 def make_shards(sizes):
@@ -621,10 +1176,6 @@
         down_weight,
     ):
         length, width = hidden_in.shape
-        groups = HEADS // KV_HEADS
-        factor = HEAD_DIM ** (-0.5)
-        x, y, c, z = (lax.axis_index(n) for n in ("x", "y", "c", "z"))
-        expert = 4 * x + 2 * y + c
         gains = jnp.stack([attn_gain, ffn_gain]).astype(F32)
         shard_rows = gains.shape[1]
         lanes = -(-shard_rows // LANES) * LANES
@@ -635,147 +1186,48 @@
         segment = segments[0]
         position = jnp.arange(length, dtype=jnp.int32)
         allowed = (position[:, None] >= position[None, :]) & (segment[:, None] == segment[None, :])
-        cosine, sine_table = rotary_tables(length, HEAD_DIM)
-        cos_wide = jnp.concatenate([cosine[:, 0], cosine[:, 0]], axis=1)
-        sin_wide = jnp.concatenate([-sine_table[:, 0], sine_table[:, 0]], axis=1)
+        cosine, sine = rotary_tables(length, HEAD_DIM)
         (
-            qkv_full, output_full, _, gate_full, up_full, down_full, rows_in, grads, shares,
-            queries, keys, value_rows, probability, attended, mixed, gain_rows,
+            wq, wo, _, gate, up, down, rows, grads, shares,
+            queries, keys, values, probability, attended, mixed, gain_rows,
         ) = forward_call(
-            depth, shard_rows, hidden_in, allowed.astype(F32), cos_wide, sin_wide, gains,
+            depth, shard_rows, hidden_in, allowed.astype(F32), cosine, sine, gains,
             wq_in, output_weight, gate_weight, up_weight, down_weight, grad_out, shares,
         )
-        gain_first, gain_second = gain_rows[0], gain_rows[1]
-        share = jnp.sum(
-            jnp.where(jnp.arange(LANES) == expert, shares, 0.0), axis=2
-        ).reshape(-1, 1)
-        rows_in, grads = rows_in.reshape(-1, width), grads.reshape(-1, width)
-        inputs = hidden_in.astype(F32)
-        normed = rms_norm(inputs, gain_first).astype(BF16)
-        probability = probability.reshape(KV_HEADS, groups, length, length)
-        probability_low = probability.astype(BF16)
-        grouped = queries.reshape(KV_HEADS, groups, length, HEAD_DIM).transpose(2, 0, 1, 3)
-        rotated_keys = keys.reshape(KV_HEADS, length, HEAD_DIM).transpose(1, 0, 2)
-        value_heads = value_rows.reshape(KV_HEADS, length, HEAD_DIM).transpose(1, 0, 2)
-        mine = 2 * y + c
-        rows = shard_rows
-        quarter = rows // 4
-        qkv = wq_in.shape[1]
-        columns = qkv + width + 128
-
-        gate_proj = dot(rows_in, gate_full, ((1,), (0,)))
-        up_proj = dot(rows_in, up_full, ((1,), (0,)))
-        sigmoid_gate = jax.nn.sigmoid(gate_proj)
-        silu_gate = gate_proj * sigmoid_gate
-        hidden_act = (silu_gate * up_proj).astype(BF16)
-        expert_grad = (share * grads.astype(F32)).astype(BF16)
-        down_grad = dot(hidden_act, expert_grad, ((0,), (0,))).astype(BF16)
-        expert_out = dot(hidden_act, down_full, ((1,), (0,)))
-        expert_part = (share * expert_out).astype(BF16).reshape(4, 2, length, width)
-        hidden_grad = dot(expert_grad, down_full, ((1,), (1,)))
-        gate_grad = (
-            hidden_grad * up_proj * sigmoid_gate * (1.0 + gate_proj * (1.0 - sigmoid_gate))
-        ).astype(BF16)
-        up_grad = (hidden_grad * silu_gate).astype(BF16)
-        rows_grad = dot(gate_grad, gate_full, ((1,), (1,))) + dot(up_grad, up_full, ((1,), (1,)))
-        rows_grad = rows_grad.astype(BF16).reshape(4, 2, length, width)
-        gate_weight_grad = dot(rows_in, gate_grad, ((0,), (0,))).astype(BF16)
-        up_weight_grad = dot(rows_in, up_grad, ((0,), (0,))).astype(BF16)
-
-        layer_out = (mixed + slab_return(expert_part)).astype(BF16)
-        normed_two_grad = slab_return(rows_grad)
-
-        def over_outer(value):
+        layer_out, grad_in, gain_total, gate_total, up_total, down_total, wq_total, wo_total = (
+            backward_call(
+                depth, shard_rows, hidden_in, grad_out, cosine, sine, gain_rows, queries, keys,
+                values, attended, mixed, probability,
+                rows.reshape(-1, width), grads.reshape(-1, width), shares,
+                gate, up, down, wq, wo,
+            )[:8]
+        )
+        z, x = lax.axis_index("z"), lax.axis_index("x")
+        gain_total = lax.dynamic_slice_in_dim(gain_total, (z * 2 + x) * shard_rows, shard_rows, 1)
+
+        def whole(value):
+            value = value.astype(F32)
             return lax.psum(value, "o") if sizes["o"] > 1 else value
 
-        def expert_scatter(grad):
-            shard = grad.shape[0] // (2 * depth)
-            blocks = grad.reshape(depth, 2, shard, grad.shape[1])
-            total = over_outer(line_scatter(blocks, depth, z)).astype(BF16)
-            own = lax.dynamic_index_in_dim(total, x, 0, keepdims=False)
-            away = lax.dynamic_index_in_dim(total, 1 - x, 0, keepdims=False)
-            four = ordered(own, swap(away, ("x",)), x)[:, None]
-            four = ordered(four, swap(four, ("y",)), y)
-            four = ordered(four, swap(four, ("c",)), c)
-            return four.transpose(2, 1, 0, 3, 4, 5).reshape(EXPERTS, shard, -1).astype(F32)
-
-        total_down = expert_scatter(down_grad)
-        total_gate = expert_scatter(gate_weight_grad)
-        total_up = expert_scatter(up_weight_grad)
-
-        upstream = grad_out.astype(F32)
-        mixed_part, ffn_gain_grad = norm_back(mixed, gain_second, normed_two_grad)
-        mixed_grad = upstream + mixed_part
-        mixed_low = mixed_grad.astype(BF16)
-        output_weight_grad = dot(attended, mixed_low, ((0,), (0,)))
-        attended_grad = dot(mixed_low, output_full, ((1,), (1,)))
-        attended_grad = attended_grad.astype(BF16).reshape(length, KV_HEADS, groups, HEAD_DIM)
-        prob_grad = jnp.einsum(
-            "ikgd,jkd->kgij", attended_grad, value_heads, preferred_element_type=F32
-        )
-        value_grad = jnp.einsum(
-            "kgij,ikgd->jkd", probability_low, attended_grad, preferred_element_type=F32
-        )
-        value_grad = value_grad.astype(BF16).reshape(length, KV_HEADS * HEAD_DIM)
-        score_grad = (
-            probability * (prob_grad - jnp.sum(probability * prob_grad, axis=-1, keepdims=True))
-        ).astype(BF16)
-        query_rot_grad = (
-            jnp.einsum("kgij,jkd->ikgd", score_grad, rotated_keys, preferred_element_type=F32)
-            * factor
-        )
-        key_rot_grad = (
-            jnp.einsum("kgij,ikgd->jkd", score_grad, grouped, preferred_element_type=F32) * factor
-        )
-        query_raw_grad = rotate(
-            query_rot_grad.reshape(length, HEADS, HEAD_DIM), cosine, -sine_table
-        )
-        query_raw_grad = query_raw_grad.astype(BF16).reshape(length, HEADS * HEAD_DIM)
-        key_raw_grad = (
-            rotate(key_rot_grad, cosine, -sine_table)
-            .astype(BF16)
-            .reshape(length, KV_HEADS * HEAD_DIM)
-        )
-        qkv_grad = jnp.concatenate([query_raw_grad, key_raw_grad, value_grad], axis=1)
-        normed_grad = dot(qkv_grad, qkv_full, ((1,), (1,)))
-        qkv_weight_grad = dot(normed, qkv_grad, ((0,), (0,)))
-        input_part, attn_gain_grad = norm_back(inputs, gain_first, normed_grad)
-        grad_in = (mixed_grad + input_part).astype(BF16)
-
-        gain_grads = jnp.stack([attn_gain_grad, ffn_gain_grad], axis=1)
-        gain_grads = jnp.pad(gain_grads, ((0, 0), (0, 126)))
-        packed_grad = jnp.concatenate(
-            [qkv_weight_grad, output_weight_grad, gain_grads], axis=1
-        ).astype(BF16)
-        parts = packed_grad.reshape(depth, 2, 2, 2, quarter, columns)
-        parts = parts.transpose(3, 1, 2, 0, 4, 5)
-
-        def pick(value, place):
-            return lax.dynamic_index_in_dim(value, place, 0, keepdims=False)
-
-        def halve(value, axis, place):
-            other = swap(pick(value, 1 - place), (axis,))
-            return (pick(value, place).astype(F32) + other.astype(F32)).astype(BF16)
-
-        parts = halve(parts, "c", c)
-        parts = halve(parts, "x", x)
-        parts = halve(parts, "y", y)
-        total = over_outer(line_scatter(parts, depth, z)).astype(BF16)
-        total = ordered(total, swap(total, ("c",)), c)
-        total = ordered(total, swap(total, ("y",)), y).reshape(rows, columns).astype(F32)
-        kv = KV_HEADS * HEAD_DIM
+        def side_by_side(value):
+            return value.transpose(1, 0, 2).reshape(shard_rows, -1)
+
+        wq_total, wo_total = side_by_side(whole(wq_total)), side_by_side(whole(wo_total))
+        queries_end = HEADS * HEAD_DIM
+        keys_end = queries_end + KV_HEADS * HEAD_DIM
+        gain_total = whole(gain_total)
         return (
             layer_out,
             grad_in,
-            total[:, qkv + width],
-            total[:, : qkv - 2 * kv],
-            total[:, qkv - 2 * kv : qkv - kv],
-            total[:, qkv - kv : qkv],
-            total[:, qkv : qkv + width],
-            total[:, qkv + width + 1],
-            total_gate,
-            total_up,
-            total_down,
+            gain_total[0],
+            wq_total[:, :queries_end],
+            wq_total[:, queries_end:keys_end],
+            wq_total[:, keys_end:],
+            wo_total,
+            gain_total[1],
+            whole(gate_total),
+            whole(up_total),
+            whole(down_total),
         )
 
     return shards

time: 684 us -> 491 us (0.72)
  Pallas kernels: 164 us -> 459 us
  waiting for transfers between devices: 168 us -> 0 us
  starting transfers between devices: 141 us -> 0 us
  matrix products: 97 us -> 0 us
  other arithmetic: 64.6 us -> 16 us
  local copies, waits for them, and re-layouts: 36.2 us -> 6.45 us
    pallas_call x0 -> x1, Pallas kernels: none -> 295 us  [backward_call(): pl.pallas_call(functools.partial(backward_kernel, depth), out_shape=out_s...]
    ppermute x46 -> x0, waiting for transfers between devices: 168 us -> none  [the longest x22 120 us: swap(): return lax.ppermute(value, axes, [(i, count - 1 - i) for i in range(count)])]
    ppermute x46 -> x0, starting transfers between devices: 141 us -> none  [the longest x22 64.3 us: swap(): return lax.ppermute(value, axes, [(i, count - 1 - i) for i in range(count)])]
    dot_general x17 -> x0, matrix products: 97 us -> none  [the longest x13 92.8 us: dot(): return lax.dot_general(a, b, (dims, ((), ())), preferred_element_type=F32)]
    convert_element_type x27 -> x3, other arithmetic: 41.4 us -> 9.85 us  [whole(): value = value.astype(F32)]
    squeeze x14 -> x0, local copies, waits for them, and re-layouts: 11.4 us -> none  [the longest x4 4.53 us: at(): lax.dynamic_index_in_dim(blocks, jnp.clip(index, 0, depth - 1), 0, keepdi...]
    add x2 -> x0, other arithmetic: 8.11 us -> none  [the longest x1 4.17 us: shards(): mixed_grad = upstream + mixed_part]
    unnamed x88 -> x24, local copies, waits for them, and re-layouts: 9.3 us -> 1.8 us
  transfers between devices with their start and end apart: 46 -> 0, of which waited for: 21 -> 0; matrix products, arithmetic and copies ran while one was open for 14% -> 0% of each run, Pallas kernels for 0% -> 0%
where the time goes in v3:
time: 491 us; the launch traced here: 483 us
  Pallas kernels  459 us (93%)
  other arithmetic  16 us (3%)
  local copies, waits for them, and re-layouts  6.45 us (1%)
    pallas_call x1, Pallas kernels, backward_call(): pl.pallas_call(functools.partial(backward_kernel, depth), out_shape=out_s...  295 us
    pallas_call x1, Pallas kernels, forward_call(): pl.pallas_call(functools.partial(forward_kernel, depth, shard_rows), out_...  164 us
    convert_element_type x3, other arithmetic, whole(): value = value.astype(F32)  9.85 us

profile of v3, /device:TPU:13, one launch (start us, length us, event | category | flops | bytes accessed | tf_op | source)
XLA Modules:
  0.0 482.8 jit_solution(7626420078270634626)
XLA Ops:
  0.6 0.0 copy-start.6
  0.7 0.0 copy-start.8
  0.7 0.0 copy-start.7
  0.7 0.0 copy-start.9
  0.7 0.5 fusion.4
  1.2 0.8 pad_maximum_fusion.1
  2.1 2.2 pad_maximum_fusion.refs_5_
  4.2 0.8 fusion.1.refs_1_
  5.0 1.0 select_reduce_fusion.refs_11_
  6.0 0.6 fusion.11.refs_4_
  6.7 164.3 %shard_map.221 = (bf16[1536,2048]{1,0:T(8,128)(2,1)}, bf16[1536,1536]{1,0:T(8,128)(2,1)}, f32[8,8,256]{2,1,0:T(8,128)}, bf16[1536,768]{1,0:T(8,128)(2,1)}, bf16[...) custom-call(bf16[256,1536]{1,0:T(8,128)(2,1)} %refs_0_.3, ...), custom_call_target="tpu_custom_call" | custom-call | tf_op jit(solution)/shard_map/pallas_call | solution.py:479
  170.9 294.8 %shard_map.222 = (bf16[256,1536]{1,0:T(8,128)(2,1)}, bf16[256,1536]{1,0:T(8,128)(2,1)}, f32[8,1536]{1,0:T(8,128)}, bf16[8,192,768]{2,1,0:T(8,128)(2,1)}, bf16[8,...) custom-call(bf16[256,1536]{1,0:T(8,128)(2,1)} %refs_0_.3, ...), custom_call_target="tpu_custom_call" | custom-call | tf_op jit(solution)/shard_map/pallas_call | solution.py:1114
  465.7 4.4 convert_element_type.18
  470.1 2.6 convert_element_type.19
  472.8 2.8 convert_element_type.20
  475.6 0.2 convert_bitcast_fusion
  475.8 0.2 copy.33
  476.0 1.1 slice.20
  477.1 0.8 fusion.12
  477.9 0.1 convert_bitcast_fusion.1
  478.0 1.2 copy.34
  479.1 1.4 fusion.13
  480.5 0.9 copy.37
  481.4 0.9 copy.38
  (21 shorter events, 0.1 us)
Async XLA Ops:
  0.6 3.6 copy-start.6
  0.7 4.4 copy-start.8
  0.7 4.4 copy-start.7
  0.7 5.3 %copy-start.9 = (bf16[192]{0:T(256)(128)(2,1)S(1)}, bf16[192]{0:T(256)(128)(2,1)}, u32[]{:S(2)}) copy-start(bf16[192]{0:T(256)(128)(2,1)} %param.24) | copy-start | bytes 1156
  0.7 5.3 %copy-start.10 = (bf16[192]{0:T(256)(128)(2,1)S(1)}, bf16[192]{0:T(256)(128)(2,1)}, u32[]{:S(2)}) copy-start(bf16[192]{0:T(256)(128)(2,1)} %param.19) | copy-start | bytes 1156
  465.7 4.4 copy-start.1
  470.1 2.6 copy-start
  472.8 2.8 copy-start.4
  476.0 1.9 copy-start.5
  477.1 3.5 copy-start.3
  478.0 3.5 copy-start.2
